TPU v7x, 256 devices: a whole 4x4x8 slice. The times are simulated.
256 devices in a mesh: seq: 32 (over z, y), prompt: 8 (over x, core).
Axes of the slice: x: 4, y: 4, z: 8, core: 2. Of those that a mesh axis runs over, the one named last changes fastest.
Arguments:
- queries: bfloat16 [65536, 1024], P(('prompt', 'seq')), parts along dimension 0, may hold values from -6 to 6
- keys: bfloat16 [65536, 1024], P(('prompt', 'seq')), parts along dimension 0, may hold values from -6 to 6
- values: bfloat16 [65536, 1024], P(('prompt', 'seq')), parts along dimension 0, may hold values from -6 to 6
- cotangent: bfloat16 [65536, 1024], P(('prompt', 'seq')), parts along dimension 0, may hold values from -6 to 6
- restrict_one: bfloat16 [8, 256], replicated, may hold values from -0.375 to 0.375
- restrict_two: bfloat16 [4, 256], replicated, may hold values from -0.375 to 0.375
Outputs:
- attended: bfloat16 [65536, 1024], P(('prompt', 'seq')), parts along dimension 0
- grad_q: bfloat16 [65536, 1024], P(('prompt', 'seq')), parts along dimension 0
- grad_k: bfloat16 [65536, 1024], P(('prompt', 'seq')), parts along dimension 0
- grad_v: bfloat16 [65536, 1024], P(('prompt', 'seq')), parts along dimension 0
There are 8 independent parts, one for each index of `prompt`. A program takes and returns all parts, laid end to end along the dimension named above; an argument that names none is the same for every part. Nothing has to cross between parts.
All inputs are finite; a program needn't handle non-finite values.
Results may differ from a plain program's by a relative error of at most 0.02.
Values may be sent and summed in bfloat16 or wider, within the bound.
A program may use at most 128 MiB of HBM per device.

v0:
```python
import math

import jax
import jax.numpy as jnp
from jax import lax
from jax.sharding import PartitionSpec as P

HEAD_DIM = 64


level_one_bias = math.log(32.0)
level_two_bias = math.log(64.0)
masked_bias = -1e30


def padded(value, sides, width):
    for axis, dim in sides:
        size, length = (lax.axis_size(axis), value.shape[dim])
        up = [(i, (i + 1) % size) for i in range(size - 1)]
        down = [(j, i) for i, j in up]
        last = lax.slice_in_dim(value, length - width, length, axis=dim)
        first = lax.slice_in_dim(value, 0, width, axis=dim)
        before = lax.ppermute(last, axis, up)
        after = lax.ppermute(first, axis, down)
        value = jnp.concatenate([before, value, after], axis=dim)
    return value


def from_behind(value, axis, by):
    size = lax.axis_size(axis)
    pairs = [(i, i + by) for i in range(size) if 0 <= i + by < size]
    return lax.ppermute(value, axis, pairs)


def key_terms(score_grad, weights, query_group, cotangent_group, lower, upper, scaling):
    grad_key = (
        jnp.einsum("hqk,qhd->khd", score_grad, query_group, preferred_element_type=jnp.float32)
        * scaling
    )
    grad_value = jnp.einsum(
        "hqk,qhd->khd", weights, cotangent_group, preferred_element_type=jnp.float32
    )
    key_count = upper - lower
    return (grad_key.reshape(key_count, -1), grad_value.reshape(key_count, -1))


def per_device(queries, keys, values, cotangent, restrict_one, restrict_two):
    row_count = queries.shape[0]
    width = queries.shape[1]
    head_count = width // HEAD_DIM
    group_size = 2
    scaling = 1.0 / math.sqrt(HEAD_DIM)
    one_rows = restrict_one.shape[0]
    two_rows = restrict_two.shape[0]
    device_count = lax.axis_size("seq")
    position = lax.axis_index("seq")
    paired = jnp.concatenate([keys, values], axis=1)
    coarse_one = jnp.dot(restrict_one, paired, preferred_element_type=jnp.float32).astype(
        jnp.bfloat16
    )
    coarse_two = jnp.dot(restrict_two, paired, preferred_element_type=jnp.float32).astype(
        jnp.bfloat16
    )
    near_keys = padded(paired, (("seq", 0),), row_count)
    received = []
    for offset in (3, 2, -2, -3):
        received.append(from_behind(coarse_one, "seq", offset))
    middle_keys = jnp.concatenate(received, axis=0)
    distant_keys = lax.all_gather(coarse_two, "seq", axis=0, tiled=True)
    key_rows = jnp.concatenate([near_keys, middle_keys, distant_keys], axis=0)
    key_count = key_rows.shape[0]
    near_place = position + jnp.repeat(jnp.array([-1, 0, 1], dtype=jnp.int32), row_count)
    middle_place = position + jnp.repeat(jnp.array([-3, -2, 2, 3], dtype=jnp.int32), one_rows)
    far_block = jnp.repeat(jnp.arange(device_count, dtype=jnp.int32), two_rows)
    key_bias = jnp.concatenate(
        [
            jnp.where((near_place >= 0) & (near_place < device_count), 0.0, masked_bias),
            jnp.where(
                (middle_place >= 0) & (middle_place < device_count), level_one_bias, masked_bias
            ),
            jnp.where(jnp.abs(far_block - position) >= 4, level_two_bias, masked_bias),
        ]
    ).astype(jnp.float32)
    query_heads = queries.reshape(row_count, head_count, HEAD_DIM)
    cotangent_heads = cotangent.reshape(row_count, head_count, HEAD_DIM)
    key_heads = key_rows[:, :width].reshape(key_count, head_count, HEAD_DIM)
    value_heads = key_rows[:, width:].reshape(key_count, head_count, HEAD_DIM)
    attended_parts = []
    grad_query_parts = []
    lse_parts = []
    delta_parts = []
    key_grad_parts = []
    value_grad_parts = []
    for group_index in range(head_count // group_size):
        lower = group_index * group_size
        upper = lower + group_size
        query_group = query_heads[:, lower:upper]
        cotangent_group = cotangent_heads[:, lower:upper]
        key_group = key_heads[:, lower:upper]
        value_group = value_heads[:, lower:upper]
        scores = (
            jnp.einsum("qhd,khd->hqk", query_group, key_group, preferred_element_type=jnp.float32)
            * scaling
            + key_bias
        )
        highest = jnp.max(scores, axis=2)
        raised = jnp.exp(scores - highest[:, :, None])
        row_total = jnp.sum(raised, axis=2)
        log_total = highest + jnp.log(row_total)
        probs = raised * (1.0 / row_total)[:, :, None]
        weights = probs.astype(jnp.bfloat16)
        attended_group = jnp.einsum(
            "hqk,khd->qhd", weights, value_group, preferred_element_type=jnp.float32
        ).astype(jnp.bfloat16)
        delta = jnp.einsum(
            "qhd,qhd->hq", cotangent_group, attended_group, preferred_element_type=jnp.float32
        )
        dots = jnp.einsum(
            "qhd,khd->hqk", cotangent_group, value_group, preferred_element_type=jnp.float32
        )
        score_grad = (probs * (dots - delta[:, :, None])).astype(jnp.bfloat16)
        grad_query = (
            jnp.einsum("hqk,khd->qhd", score_grad, key_group, preferred_element_type=jnp.float32)
            * scaling
        )
        attended_parts.append(attended_group.reshape(row_count, -1))
        grad_query_parts.append(grad_query.reshape(row_count, -1))
        lse_parts.append(log_total)
        delta_parts.append(delta)
        grad_key, grad_value = key_terms(
            score_grad, weights, query_group, cotangent_group, 0, key_count, scaling
        )
        key_grad_parts.append(grad_key)
        value_grad_parts.append(grad_value)
    attended = jnp.concatenate(attended_parts, axis=1)
    grad_q = jnp.concatenate(grad_query_parts, axis=1).astype(jnp.bfloat16)
    all_grads = jnp.concatenate(
        [jnp.concatenate(key_grad_parts, axis=1), jnp.concatenate(value_grad_parts, axis=1)], axis=1
    )
    own_grads = all_grads[row_count : 2 * row_count]
    for offset, piece in (
        (1, all_grads[2 * row_count : 3 * row_count]),
        (-1, all_grads[:row_count]),
    ):
        own_grads = own_grads + from_behind(piece.astype(jnp.bfloat16), "seq", offset).astype(
            piece.dtype
        )
    coarse_grads = all_grads[3 * row_count :]
    middle_sum = jnp.zeros((one_rows, 2 * width), jnp.float32)
    for slot, offset in enumerate((3, 2, -2, -3)):
        piece = coarse_grads[slot * one_rows : (slot + 1) * one_rows]
        middle_sum = middle_sum + from_behind(piece.astype(jnp.bfloat16), "seq", -offset).astype(
            piece.dtype
        )
    far_sum = lax.psum_scatter(
        coarse_grads[4 * one_rows :].astype(jnp.bfloat16), "seq", scatter_dimension=0, tiled=True
    ).astype(jnp.float32)
    total = own_grads + jnp.dot(
        restrict_one.astype(jnp.float32).T, middle_sum, precision=lax.Precision.HIGHEST
    )
    total = total + jnp.dot(
        restrict_two.astype(jnp.float32).T, far_sum, precision=lax.Precision.HIGHEST
    )
    return (
        attended,
        grad_q,
        total[:, :width].astype(jnp.bfloat16),
        total[:, width:].astype(jnp.bfloat16),
    )


def solution(mesh):
    in_specs = (
        P(("prompt", "seq"), None),
        P(("prompt", "seq"), None),
        P(("prompt", "seq"), None),
        P(("prompt", "seq"), None),
        P(),
        P(),
    )
    out_specs = (
        P(("prompt", "seq"), None),
        P(("prompt", "seq"), None),
        P(("prompt", "seq"), None),
        P(("prompt", "seq"), None),
    )
    return jax.shard_map(
        per_device, mesh=mesh, in_specs=in_specs, out_specs=out_specs, check_vma=False
    )
```

profile of v0, /device:TPU:2, one launch (start us, length us, event | category | flops | bytes accessed | tf_op | source)
XLA Modules:
  0.0 443.7 jit_solution(2547696244742269014)
XLA Ops:
  9.4 4.6 %collective-permute-start = (bf16[256,2048]{1,0:T(8,128)(2,1)S(1)}, bf16[256,2048]{1,0:T(8,128)(2,1)}, u32[]{:S(2)}, u32[]{:S(2)}) collective-permute-start(bf16[256,2048]{1,0:T(8,128)(2,1)S(1)} %constant_dynamic-update-slice_fusion), channel_id=1, source_target_pairs={{0,8},{8,16},{16,24},{24,32},{32,40},{40,48},{48,56},{56,64},{64,7... | collective-permute-start | bytes 3145736 | tf_op jit(solution)/shard_map/ppermute | solution.py:23
  15.6 5.1 %collective-permute-start.2 = (bf16[8,2048]{1,0:T(8,128)(2,1)S(1)}, bf16[8,2048]{1,0:T(8,128)(2,1)S(1)}, u32[]{:S(2)}, u32[]{:S(2)}) collective-permute-start(bf16[8,2048]{1,0:T(8,128)(2,1)S(1)} %fusion.8), channel_id=1, source_target_pairs={{0,24},{8,32},{16,40},{24,48},{32,56},{40,64},{48,72},{56,80},{64,... | collective-permute-start | bytes 98312 | tf_op jit(solution)/shard_map/ppermute | solution.py:32
  20.7 3.9 collective-permute-start.3
  26.2 63.7 %all-gather = bf16[32,4,2048]{2,1,0:T(4,128)(2,1)S(1)} all-gather(bf16[1,4,2048]{2,1,0:T(4,128)(2,1)S(1)} %fusion.9), channel_id=1, replica_groups=mesh['seq'=32,'prompt'=8] {'seq'}, dimensions={0}, use_global_device_ids=true | all-gather | bytes 540672 | tf_op jit(solution)/shard_map/all_gather | solution.py:69
  120.3 4.3 copy.117
  124.6 4.1 fusion.270
  136.7 4.1 fusion.272
  143.9 4.1 fusion.273
  151.0 4.0 fusion.274
  158.0 4.1 fusion.275
  165.7 4.0 fusion.276
  173.8 4.0 fusion.277
  178.4 4.2 fusion.151
  203.7 3.7 fusion.79
  211.1 3.8 fusion.97
  214.9 3.7 fusion.106
  218.7 3.7 fusion.115
  222.4 3.7 fusion.124
  226.1 3.8 fusion.133
  229.9 4.1 fusion.142
  262.8 3.7 convert.61
  282.3 4.6 %collective-permute-start.6 = (bf16[256,2048]{1,0:T(8,128)(2,1)S(1)}, bf16[256,2048]{1,0:T(8,128)(2,1)S(1)}, u32[]{:S(2)}, u32[]{:S(2)}) collective-permute-start(bf16[256,2048]{1,0:T(8,128)(2,1)S(1)} %get-tuple-element.28), channel_id=1, source_target_pairs={{0,8},{8,16},{16,24},{24,32},{32,40},{40,48},{48,56},{56,64},{64,7... | collective-permute-start | bytes 3145736 | tf_op jit(solution)/shard_map/ppermute | solution.py:32
  286.9 6.3 %collective-permute-start.11 = (bf16[8,2048]{1,0:T(8,128)(2,1)}, bf16[8,2048]{1,0:T(8,128)(2,1)}, u32[]{:S(2)}, u32[]{:S(2)}) collective-permute-start(bf16[8,2048]{1,0:T(8,128)(2,1)} %get-tuple-element.25), channel_id=1, source_target_pairs={{0,24},{8,32},{16,40},{24,48},{32,56},{40,64},{48,72},{56,80},{64,... | collective-permute-start | bytes 98312 | tf_op jit(solution)/shard_map/ppermute | solution.py:32
  312.3 118.5 %all-reduce.3.cloned.1.call-done = bf16[128,2048]{0,1:T(8,128)(2,1)} async-done(((bf16[128,2048]{0,1:T(8,128)(2,1)}), bf16[128,2048]{0,1:T(8,128)(2,1)}) %all-reduce.3.cloned.1.call-update) | async-done | bytes 524304
  (327 shorter events, 153.7 us)
Async XLA Ops:
  7.2 423.6 %all-reduce.3.cloned.1.call-start = ((), (), s32[]{:S(2)}) async-start(), calls=%async_computation | async-start | bytes 1048576
  9.4 81.4 %copy-start.28 = (bf16[256,1024]{1,0:T(8,128)(2,1)S(1)}, bf16[256,1024]{1,0:T(8,128)(2,1)}, u32[]{:S(2)}) copy-start(bf16[256,1024]{1,0:T(8,128)(2,1)} %param.8) | copy-start | bytes 1572868
  9.4 84.6 %collective-permute-start = (bf16[256,2048]{1,0:T(8,128)(2,1)S(1)}, bf16[256,2048]{1,0:T(8,128)(2,1)}, u32[]{:S(2)}, u32[]{:S(2)}) collective-permute-start(bf16[256,2048]{1,0:T(8,128)(2,1)S(1)} %constant_dynamic-update-slice_fusion), channel_id=1, source_target_pairs={{0,8},{8,16},{16,24},{24,32},{32,40},{40,48},{48,56},{56,64},{64,7... | collective-permute-start | bytes 3145736 | tf_op jit(solution)/shard_map/ppermute | solution.py:23
  14.0 82.7 %collective-permute-start.1 = (bf16[256,2048]{1,0:T(8,128)(2,1)S(1)}, bf16[256,2048]{1,0:T(8,128)(2,1)}, u32[]{:S(2)}, u32[]{:S(2)}) collective-permute-start(bf16[256,2048]{1,0:T(8,128)(2,1)S(1)} %constant_dynamic-update-slice_fusion), channel_id=1, source_target_pairs={{8,0},{16,8},{24,16},{32,24},{40,32},{48,40},{56,48},{64,56},{72,6... | collective-permute-start | bytes 3145736 | tf_op jit(solution)/shard_map/ppermute | solution.py:24
  15.6 75.5 %copy-start.78 = (s32[4]{0:T(128)S(1)}, s32[4]{0:T(128)}, u32[]{:S(2)}) copy-start(s32[4]{0:T(128)} %constant.13.clone) | copy-start | bytes 52
  15.6 75.7 %copy-start.77 = (s32[3]{0:T(128)S(1)}, s32[3]{0:T(128)}, u32[]{:S(2)}) copy-start(s32[3]{0:T(128)} %constant.12.clone) | copy-start | bytes 40
  15.6 82.6 %collective-permute-start.2 = (bf16[8,2048]{1,0:T(8,128)(2,1)S(1)}, bf16[8,2048]{1,0:T(8,128)(2,1)S(1)}, u32[]{:S(2)}, u32[]{:S(2)}) collective-permute-start(bf16[8,2048]{1,0:T(8,128)(2,1)S(1)} %fusion.8), channel_id=1, source_target_pairs={{0,24},{8,32},{16,40},{24,48},{32,56},{40,64},{48,72},{56,80},{64,... | collective-permute-start | bytes 98312 | tf_op jit(solution)/shard_map/ppermute | solution.py:32
  20.7 77.4 %collective-permute-start.3 = (bf16[8,2048]{1,0:T(8,128)(2,1)S(1)}, bf16[8,2048]{1,0:T(8,128)(2,1)S(1)}, u32[]{:S(2)}, u32[]{:S(2)}) collective-permute-start(bf16[8,2048]{1,0:T(8,128)(2,1)S(1)} %fusion.8), channel_id=1, source_target_pairs={{0,16},{8,24},{16,32},{24,40},{32,48},{40,56},{48,64},{56,72},{64,... | collective-permute-start | bytes 98312 | tf_op jit(solution)/shard_map/ppermute | solution.py:32
  24.6 73.6 %collective-permute-start.4 = (bf16[8,2048]{1,0:T(8,128)(2,1)S(1)}, bf16[8,2048]{1,0:T(8,128)(2,1)S(1)}, u32[]{:S(2)}, u32[]{:S(2)}) collective-permute-start(bf16[8,2048]{1,0:T(8,128)(2,1)S(1)} %fusion.8), channel_id=1, source_target_pairs={{16,0},{24,8},{32,16},{40,24},{48,32},{56,40},{64,48},{72,56},{80,... | collective-permute-start | bytes 98312 | tf_op jit(solution)/shard_map/ppermute | solution.py:32
  26.2 66.5 %copy-start.76 = (u32[256]{0:T(256)S(1)}, u32[256]{0:T(256)}, u32[]{:S(2)}) copy-start(u32[256]{0:T(256)} %constant.46) | copy-start | bytes 3076
  94.0 7.0 %collective-permute-start.5 = (bf16[8,2048]{1,0:T(8,128)(2,1)S(1)}, bf16[8,2048]{1,0:T(8,128)(2,1)S(1)}, u32[]{:S(2)}, u32[]{:S(2)}) collective-permute-start(bf16[8,2048]{1,0:T(8,128)(2,1)S(1)} %fusion.8), channel_id=1, source_target_pairs={{24,0},{32,8},{40,16},{48,24},{56,32},{64,40},{72,48},{80,56},{88,... | collective-permute-start | bytes 98312 | tf_op jit(solution)/shard_map/ppermute | solution.py:32
  133.6 44.7 %copy-start.45 = (bf16[2,64,256]{2,1,0:T(8,128)(2,1)}, bf16[2,64,256]{2,1,0:T(8,128)(2,1)S(1)}, u32[]{:S(2)}) copy-start(bf16[2,64,256]{2,1,0:T(8,128)(2,1)S(1)} %convolution_convert_fusion.9) | copy-start | bytes 196612
  136.7 41.7 %copy-start.43 = (bf16[2,64,256]{2,1,0:T(8,128)(2,1)}, bf16[2,64,256]{2,1,0:T(8,128)(2,1)S(1)}, u32[]{:S(2)}) copy-start(bf16[2,64,256]{2,1,0:T(8,128)(2,1)S(1)} %convolution_convert_fusion.8) | copy-start | bytes 196612
  143.9 34.5 %copy-start.47 = (bf16[2,64,256]{2,1,0:T(8,128)(2,1)}, bf16[2,64,256]{2,1,0:T(8,128)(2,1)S(1)}, u32[]{:S(2)}) copy-start(bf16[2,64,256]{2,1,0:T(8,128)(2,1)S(1)} %convolution_convert_fusion.7) | copy-start | bytes 196612
  151.0 27.3 %copy-start.49 = (bf16[2,64,256]{2,1,0:T(8,128)(2,1)}, bf16[2,64,256]{2,1,0:T(8,128)(2,1)S(1)}, u32[]{:S(2)}) copy-start(bf16[2,64,256]{2,1,0:T(8,128)(2,1)S(1)} %convolution_convert_fusion.6) | copy-start | bytes 196612
  275.5 26.2 %copy-start.39 = (bf16[256,128]{1,0:T(8,128)(2,1)S(1)}, bf16[256,128]{1,0:T(8,128)(2,1)}, u32[]{:S(2)}) copy-start(bf16[256,128]{1,0:T(8,128)(2,1)} %copy.126) | copy-start | bytes 196612
  276.8 24.2 %copy-start.40 = (bf16[256,128]{1,0:T(8,128)(2,1)S(1)}, bf16[256,128]{1,0:T(8,128)(2,1)}, u32[]{:S(2)}) copy-start(bf16[256,128]{1,0:T(8,128)(2,1)} %copy.125) | copy-start | bytes 196612
  277.6 22.8 %copy-start.41 = (bf16[256,128]{1,0:T(8,128)(2,1)S(1)}, bf16[256,128]{1,0:T(8,128)(2,1)}, u32[]{:S(2)}) copy-start(bf16[256,128]{1,0:T(8,128)(2,1)} %copy.124) | copy-start | bytes 196612
  281.0 151.4 %collective-permute-start.7 = (bf16[256,2048]{1,0:T(8,128)(2,1)}, bf16[256,2048]{1,0:T(8,128)(2,1)S(1)}, u32[]{:S(2)}, u32[]{:S(2)}) collective-permute-start(bf16[256,2048]{1,0:T(8,128)(2,1)} %get-tuple-element.29), channel_id=1, source_target_pairs={{8,0},{16,8},{24,16},{32,24},{40,32},{48,40},{56,48},{64,56},{72,6... | collective-permute-start | bytes 3145736 | tf_op jit(solution)/shard_map/ppermute | solution.py:32
  282.3 150.1 %collective-permute-start.6 = (bf16[256,2048]{1,0:T(8,128)(2,1)S(1)}, bf16[256,2048]{1,0:T(8,128)(2,1)S(1)}, u32[]{:S(2)}, u32[]{:S(2)}) collective-permute-start(bf16[256,2048]{1,0:T(8,128)(2,1)S(1)} %get-tuple-element.28), channel_id=1, source_target_pairs={{0,8},{8,16},{16,24},{24,32},{32,40},{40,48},{48,56},{56,64},{64,7... | collective-permute-start | bytes 3145736 | tf_op jit(solution)/shard_map/ppermute | solution.py:32
  286.9 24.0 %collective-permute-start.11 = (bf16[8,2048]{1,0:T(8,128)(2,1)}, bf16[8,2048]{1,0:T(8,128)(2,1)}, u32[]{:S(2)}, u32[]{:S(2)}) collective-permute-start(bf16[8,2048]{1,0:T(8,128)(2,1)} %get-tuple-element.25), channel_id=1, source_target_pairs={{0,24},{8,32},{16,40},{24,48},{32,56},{40,64},{48,72},{56,80},{64,... | collective-permute-start | bytes 98312 | tf_op jit(solution)/shard_map/ppermute | solution.py:32
  293.3 139.1 %collective-permute-start.10 = (bf16[8,2048]{1,0:T(8,128)(2,1)}, bf16[8,2048]{1,0:T(8,128)(2,1)}, u32[]{:S(2)}, u32[]{:S(2)}) collective-permute-start(bf16[8,2048]{1,0:T(8,128)(2,1)} %get-tuple-element.26), channel_id=1, source_target_pairs={{0,16},{8,24},{16,32},{24,40},{32,48},{40,56},{48,64},{56,72},{64,... | collective-permute-start | bytes 98312 | tf_op jit(solution)/shard_map/ppermute | solution.py:32
  295.5 136.9 %collective-permute-start.9 = (bf16[8,2048]{1,0:T(8,128)(2,1)}, bf16[8,2048]{1,0:T(8,128)(2,1)}, u32[]{:S(2)}, u32[]{:S(2)}) collective-permute-start(bf16[8,2048]{1,0:T(8,128)(2,1)} %get-tuple-element.27), channel_id=1, source_target_pairs={{16,0},{24,8},{32,16},{40,24},{48,32},{56,40},{64,48},{72,56},{80,... | collective-permute-start | bytes 98312 | tf_op jit(solution)/shard_map/ppermute | solution.py:32
  311.0 121.4 %collective-permute-start.8 = (bf16[8,2048]{1,0:T(8,128)(2,1)}, bf16[8,2048]{1,0:T(8,128)(2,1)S(1)}, u32[]{:S(2)}, u32[]{:S(2)}) collective-permute-start(bf16[8,2048]{1,0:T(8,128)(2,1)} %get-tuple-element.24), channel_id=1, source_target_pairs={{24,0},{32,8},{40,16},{48,24},{56,32},{64,40},{72,48},{80,56},{88,... | collective-permute-start | bytes 98312 | tf_op jit(solution)/shard_map/ppermute | solution.py:32
  (69 other events, 347.4 us)
Sparse Core Ops, SparseCore 0:
  281.1 149.5 all-reduce.2
where the time goes:
time: 450 us; the launch traced here: 444 us
  waiting for transfers between devices  121 us (27%)
  matrix products  96 us (21%)
  local copies, waits for them, and re-layouts  76.3 us (17%)
  blocking collectives  63.7 us (14%)
  other arithmetic  35.8 us (8%)
  starting transfers between devices  34.5 us (8%)
  between operations  16.1 us (4%)
    unnamed x2, waiting for transfers between devices  119 us
    all_gather x1, blocking collectives, per_device(): distant_keys = lax.all_gather(coarse_two, 'seq', axis=0, tiled=True)  63.7 us
    unnamed x200, local copies, waits for them, and re-layouts  37.5 us
    dot_general x8, matrix products, key_terms(): jnp.einsum('hqk,qhd->khd', weights, cotangent_group, preferred_element_ty...  30.3 us
    sub x8, other arithmetic, per_device(): raised = jnp.exp(scores - highest[:, :, None])  30.2 us
    ppermute x10, starting transfers between devices, from_behind(): return lax.ppermute(value, axis, pairs)  28.6 us
    dot_general x8, matrix products, per_device(): jnp.einsum('hqk,khd->qhd', weights, value_group, preferred_element_type=j...  25.9 us
    dot_general x8, matrix products, per_device(): jnp.einsum('qhd,khd->hqk', query_group, key_group, preferred_element_type...  13.9 us
  transfers between devices with their start and end apart: 13, of which 2 were waited for; matrix products, arithmetic and copies ran while one was open for 5% of the time, Pallas kernels for 0%

commit v1 on v0

v1 whole, which is shorter than its diff:
```python
import functools
import math

import jax
import jax.numpy as jnp
from jax import lax
from jax.experimental import pallas as pl
from jax.experimental.pallas import tpu as pltpu
from jax.sharding import PartitionSpec as P

HEAD_DIM = 64
ROWS = 256
PAIR = 128
Y = 4
Z = 8
BLOCKS = Y * Z
ONE = 8
TWO = 4
MID = (-3, -2, 2, 3)
MID_ROWS = len(MID) * ONE
FAR_ROWS = (Z - 1) * Y * TWO
COARSE = MID_ROWS + FAR_ROWS
NEAR = 3 * ROWS
KEYS = NEAR + COARSE
PADDED = 4 * ROWS
CHUNK = 48
MASKED = -1e30
F32 = jnp.float32
BF16 = jnp.bfloat16
MESH = pl.DeviceIdType.MESH


def dot(a, b, ca, cb):
    return lax.dot_general(a, b, (((ca,), (cb,)), ((), ())), preferred_element_type=F32)


def group_max(x):
    return jnp.max(x.reshape(x.shape[0] // 8, 8, x.shape[1]), axis=0)


def group_sum(x):
    return jnp.sum(x.reshape(x.shape[0] // 8, 8, x.shape[1]), axis=0)


def kernel(
    groups, parts,
    q_hbm, k_hbm, v_hbm, do_hbm, r1_ref, r2_ref,
    att_hbm, gq_hbm, gk_hbm, gv_hbm,
    own_in, near_kv, near_send, near_recv, own_grad, coarse,
    c1_send, c1_recv, c2_send, c2_recv, z_send, mg_send, mg_recv, fg_send, fg_recv, yg_send, yg_recv,
    restrict, pack, gathered, bias, q_stack, do_stack, key_t, value_t, do_t, score, dots, prob, grad,
    att_t, gq_t, stage, coarse_sum, restrict_t,
    load_sem, near_send_sem, near_recv_sem, grad_send_sem, grad_recv_sem,
    c1_send_sem, c1_recv_sem, c2_send_sem, c2_recv_sem, z_send_sem, z_recv_sem,
    mg_send_sem, mg_recv_sem, fg_send_sem, fg_recv_sem, yg_send_sem, yg_recv_sem, out_sem,
):
    width = groups * PAIR
    half = width // 2
    part_groups = groups // parts
    part_width = width // parts
    me = lax.axis_index("seq")
    z = me // Y
    y = me % Y

    def at_block(offset):
        return lax.rem(me + offset + BLOCKS, BLOCKS)

    def at_y(offset):
        return z * Y + lax.rem(y + offset + Y, Y)

    def at_z(offset):
        return lax.rem(z + offset + Z, Z) * Y + y

    def remote(src, dst, send_sem, recv_sem, to):
        return pltpu.make_async_remote_copy(
            src_ref=src, dst_ref=dst, send_sem=send_sem, recv_sem=recv_sem,
            device_id={"seq": to}, device_id_type=MESH,
        )

    def columns(index, size):
        return pl.ds(pl.multiple_of(index * size, size), size)

    loads = [
        pltpu.make_async_copy(src, own_in.at[i], load_sem.at[i])
        for i, src in enumerate((k_hbm, v_hbm, q_hbm, do_hbm))
    ]
    for load in loads:
        load.start()

    barrier = pltpu.get_barrier_semaphore()
    partners = [at_block(o) for o in (-1, 1) + MID]
    partners += [at_y(j) for j in range(1, Y)] + [at_z(k) for k in range(1, Z)]
    for partner in partners:
        pl.semaphore_signal(barrier, inc=1, device_id={"seq": partner}, device_id_type=MESH)
    pl.semaphore_wait(barrier, len(partners))

    def near_copy(side, which, g):
        src = (k_hbm, v_hbm)[which].at[:, columns(g, PAIR)]
        return remote(
            src, near_kv.at[side, g, pl.ds(which * ROWS, ROWS)],
            near_send_sem.at[side, which, g], near_recv_sem.at[side, which, g],
            at_block(1 if side == 0 else -1),
        )

    def send_near(g, carry):
        for side in range(2):
            for which in range(2):
                near_copy(side, which, g).start()
        return carry

    lax.fori_loop(0, groups, send_near, 0)

    restrict[...] = jnp.zeros_like(restrict)
    restrict[0:ONE, :] = r1_ref[...].astype(F32)
    restrict[ONE:ONE + TWO, :] = r2_ref[...].astype(F32)
    restrict_b = restrict[...].astype(BF16)
    restrict_t[...] = restrict[...].T.astype(BF16)
    loads[0].wait()
    loads[1].wait()
    coarse_k = dot(restrict_b, own_in[0], 1, 0)
    coarse_v = dot(restrict_b, own_in[1], 1, 0)
    gathered[0] = coarse_k
    gathered[1] = coarse_v

    def pack_rows(first):
        for which in range(2):
            for side in range(2):
                row = TWO * (2 * which + side)
                pack[row:row + TWO, :] = gathered[which, first:first + TWO, side * half:(side + 1) * half]
        return pack[...].astype(BF16)

    c2_send[...] = pack_rows(ONE)
    c2_copies = [
        remote(c2_send, c2_recv.at[j - 1], c2_send_sem.at[j - 1], c2_recv_sem.at[j - 1], at_y(j))
        for j in range(1, Y)
    ]
    for copy in c2_copies:
        copy.start()
    c1_send[...] = jnp.concatenate([coarse_k[0:ONE], coarse_v[0:ONE]], axis=0).astype(BF16)
    c1_copies = [
        remote(c1_send, c1_recv.at[s], c1_send_sem.at[s], c1_recv_sem.at[s], at_block(-o))
        for s, o in enumerate(MID)
    ]
    for copy in c1_copies:
        copy.start()

    row = lax.broadcasted_iota(jnp.int32, (COARSE, ROWS), 0)
    slot = row >> 3
    offset = jnp.where(slot == 0, -3, jnp.where(slot == 1, -2, jnp.where(slot == 2, 2, 3)))
    place = me + offset
    middle = jnp.where((place >= 0) & (place < BLOCKS), math.log(32.0), MASKED)
    far_row = row - MID_ROWS
    far_z = (z - 1 - (far_row >> 4)) & (Z - 1)
    far_y = (y - ((far_row >> 2) & 3)) & (Y - 1)
    distance = jnp.abs(far_z * Y + far_y - me)
    far = jnp.where(distance >= 4, math.log(64.0), MASKED)
    bias[...] = jnp.where(row < MID_ROWS, middle, far)
    left_bias = jnp.where(me >= 1, 0.0, MASKED).astype(F32)
    right_bias = jnp.where(me < BLOCKS - 1, 0.0, MASKED).astype(F32)
    for which in range(2):
        coarse[which, COARSE:ROWS, :] = jnp.zeros((ROWS - COARSE, width), BF16)
    prob[KEYS:PADDED, :] = jnp.zeros((PADDED - KEYS, 2 * ROWS), BF16)
    grad[KEYS:PADDED, :] = jnp.zeros((PADDED - KEYS, 2 * ROWS), BF16)

    for j in range(Y):
        if j == 0:
            block = c2_send[...]
        else:
            c2_copies[j - 1].wait_recv()
            block = c2_recv[j - 1]
        pack[...] = block.astype(F32)
        for which in range(2):
            for side in range(2):
                first = TWO * (2 * which + side)
                gathered[which, TWO * j:TWO * (j + 1), side * half:(side + 1) * half] = pack[first:first + TWO, :]
    z_send[...] = gathered[...].astype(BF16)

    def z_copy(k, part):
        cols = columns(part, part_width)
        return remote(
            z_send.at[:, :, cols],
            coarse.at[:, pl.ds(MID_ROWS + (k - 1) * Y * TWO, Y * TWO), cols],
            z_send_sem.at[part, k - 1], z_recv_sem.at[part, k - 1], at_z(k),
        )

    for part in range(parts):
        for k in range(1, Z):
            z_copy(k, part).start()

    for copy in c1_copies:
        copy.wait_recv()
    for which in range(2):
        rows = [c1_recv[s].astype(F32)[which * ONE:(which + 1) * ONE] for s in range(len(MID))]
        coarse[which, 0:MID_ROWS, :] = jnp.concatenate(rows, axis=0).astype(BF16)
    loads[2].wait()
    loads[3].wait()

    def grad_copy(side, g):
        return remote(
            near_send.at[side, g], near_recv.at[1 - side, g],
            grad_send_sem.at[side, g], grad_recv_sem.at[1 - side, g],
            at_block(-1 if side == 0 else 1),
        )

    def mg_copy(s, part):
        cols = columns(part, part_width)
        return remote(
            mg_send.at[s, :, cols], mg_recv.at[s, :, cols],
            mg_send_sem.at[part, s], mg_recv_sem.at[part, s], at_block(MID[s]),
        )

    def fg_copy(k, part):
        cols = columns(part, part_width)
        return remote(
            fg_send.at[k - 1, :, :, cols], fg_recv.at[k - 1, :, :, cols],
            fg_send_sem.at[part, k - 1], fg_recv_sem.at[part, k - 1], at_z(-k),
        )

    def out_copy(which, g):
        out = (att_hbm, gq_hbm, gk_hbm, gv_hbm)[which]
        return pltpu.make_async_copy(stage.at[which, g], out.at[:, columns(g, PAIR)], out_sem.at[which, g])

    def pair(g, carry):
        cols = columns(g, PAIR)
        part = g // part_groups

        @pl.when(g % part_groups == 0)
        def _():
            for k in range(1, Z):
                z_copy(k, part).wait_recv()

        for side in range(2):
            for which in range(2):
                near_copy(side, which, g).wait_recv()

        def key_value(which):
            first = which * ROWS
            return (
                near_kv[0, g, first:first + ROWS, :],
                own_in[which, :, cols],
                near_kv[1, g, first:first + ROWS, :],
                coarse[which, :, cols],
            )

        q = own_in[2, :, cols].astype(F32) * (1.0 / math.sqrt(HEAD_DIM))
        do = own_in[3, :, cols].astype(F32)
        lane = lax.broadcasted_iota(jnp.int32, (ROWS, PAIR), 1)
        for h in range(2):
            mine = (lane >= HEAD_DIM) if h else (lane < HEAD_DIM)
            q_stack[h * ROWS:(h + 1) * ROWS, :] = jnp.where(mine, q, 0.0).astype(BF16)
            do_stack[h * ROWS:(h + 1) * ROWS, :] = jnp.where(mine, do, 0.0).astype(BF16)
        do_t[...] = do.T
        keys = key_value(0)
        values = key_value(1)
        for i in range(4):
            key_t[:, i * ROWS:(i + 1) * ROWS] = keys[i].T
            value_t[:, i * ROWS:(i + 1) * ROWS] = values[i].T
        counts = (ROWS, ROWS, ROWS, COARSE)
        biases = (left_bias, None, right_bias, bias)
        for h in range(2):
            qh = q_stack[h * ROWS:(h + 1) * ROWS, :]
            doh = do_stack[h * ROWS:(h + 1) * ROWS, :]
            lanes = slice(h * ROWS, (h + 1) * ROWS)
            top = None
            for i in range(4):
                n = counts[i]
                s = dot(keys[i][:n], qh, 1, 1)
                if i == 3:
                    s = s + bias[...]
                elif biases[i] is not None:
                    s = s + biases[i]
                score[h, i * ROWS:i * ROWS + n, :] = s
                m = group_max(s)
                top = m if top is None else jnp.maximum(top, m)
                dots[h, i * ROWS:i * ROWS + n, :] = dot(values[i][:n], doh, 1, 1)
            top = jnp.max(top, axis=0, keepdims=True)
            total = jnp.zeros((8, ROWS), F32)
            for c in range(0, KEYS, CHUNK):
                p = jnp.exp(score[h, c:c + CHUNK, :] - top)
                score[h, c:c + CHUNK, :] = p
                total = total + group_sum(p)
            inverse = 1.0 / jnp.sum(total, axis=0, keepdims=True)
            for c in range(0, KEYS, CHUNK):
                p = score[h, c:c + CHUNK, :] * inverse
                prob[c:c + CHUNK, lanes] = p.astype(BF16)
            head = slice(h * HEAD_DIM, (h + 1) * HEAD_DIM)
            att = dot(value_t[head, :], prob[:, lanes], 1, 0).astype(BF16).astype(F32)
            att_t[head, :] = att
            delta = jnp.sum(att * do_t[head, :], axis=0, keepdims=True)
            for c in range(0, KEYS, CHUNK):
                p = score[h, c:c + CHUNK, :] * inverse
                grad[c:c + CHUNK, lanes] = (p * (dots[h, c:c + CHUNK, :] - delta)).astype(BF16)
            gq_t[head, :] = dot(key_t[head, :], grad[:, lanes], 1, 0) * (1.0 / math.sqrt(HEAD_DIM))
        stage[0, g] = att_t[...].T.astype(BF16)
        stage[1, g] = gq_t[...].T.astype(BF16)
        out_copy(0, g).start()
        out_copy(1, g).start()

        def key_grads(first, n):
            return (
                dot(grad[first:first + n, :], q_stack[...], 1, 0),
                dot(prob[first:first + n, :], do_stack[...], 1, 0),
            )

        for side in range(2):
            dk, dv = key_grads(2 * ROWS * side, ROWS)
            near_send[side, g, 0:ROWS, :] = dk.astype(BF16)
            near_send[side, g, ROWS:2 * ROWS, :] = dv.astype(BF16)
            grad_copy(side, g).start()
        dk, dv = key_grads(ROWS, ROWS)
        own_grad[g, 0:ROWS, :] = dk
        own_grad[g, ROWS:2 * ROWS, :] = dv
        dk, dv = key_grads(NEAR, COARSE)
        for s in range(len(MID)):
            both = jnp.concatenate([dk[s * ONE:(s + 1) * ONE], dv[s * ONE:(s + 1) * ONE]], axis=0)
            mg_send[s, :, cols] = both.astype(BF16)
        for k in range(1, Z):
            first = MID_ROWS + (k - 1) * Y * TWO
            fg_send[k - 1, 0, :, cols] = dk[first:first + Y * TWO].astype(BF16)
            fg_send[k - 1, 1, :, cols] = dv[first:first + Y * TWO].astype(BF16)

        @pl.when(g % part_groups == part_groups - 1)
        def _():
            for k in range(1, Z):
                fg_copy(k, part).start()
            for s in range(len(MID)):
                mg_copy(s, part).start()

        return carry

    lax.fori_loop(0, groups, pair, 0)

    for part in range(parts):
        for k in range(1, Z):
            fg_copy(k, part).wait_recv()
    for which in range(2):
        total = fg_recv[0, which].astype(F32)
        for k in range(2, Z):
            total = total + fg_recv[k - 1, which].astype(F32)
        gathered[which] = total
    yg_copies = [
        remote(yg_send.at[j - 1], yg_recv.at[j - 1], yg_send_sem.at[j - 1], yg_recv_sem.at[j - 1], at_y(-j))
        for j in range(1, Y)
    ]
    for j in range(1, Y):
        yg_send[j - 1] = pack_rows(TWO * j)
        yg_copies[j - 1].start()
    for part in range(parts):
        for s in range(len(MID)):
            mg_copy(s, part).wait_recv()
    middle_sum = mg_recv[0].astype(F32)
    for s in range(1, len(MID)):
        middle_sum = middle_sum + mg_recv[s].astype(F32)
    coarse_sum[...] = jnp.zeros_like(coarse_sum)
    for which in range(2):
        coarse_sum[which, 0:ONE, :] = middle_sum[which * ONE:(which + 1) * ONE]
        coarse_sum[which, ONE:ONE + TWO, :] = gathered[which, 0:TWO, :]
    for j in range(1, Y):
        yg_copies[j - 1].wait_recv()
        pack[...] = yg_recv[j - 1].astype(F32)
        for which in range(2):
            for side in range(2):
                first = TWO * (2 * which + side)
                cols = slice(side * half, (side + 1) * half)
                coarse_sum[which, ONE:ONE + TWO, cols] = (
                    coarse_sum[which, ONE:ONE + TWO, cols] + pack[first:first + TWO, :]
                )

    def finish(g, carry):
        cols = columns(g, PAIR)
        for side in range(2):
            grad_copy(side, g).wait_recv()
        for which in range(2):
            rows = slice(which * ROWS, (which + 1) * ROWS)
            wide = coarse_sum[which, :, cols]
            high = wide.astype(BF16)
            low = (wide - high.astype(F32)).astype(BF16)
            total = own_grad[g, rows, :] + dot(restrict_t[...], high, 1, 0) + dot(restrict_t[...], low, 1, 0)
            total = total + near_recv[0, g, rows, :].astype(F32) + near_recv[1, g, rows, :].astype(F32)
            stage[2 + which, g] = total.astype(BF16)
            out_copy(2 + which, g).start()
        return carry

    lax.fori_loop(0, groups, finish, 0)

    def drain(g, carry):
        for side in range(2):
            for which in range(2):
                near_copy(side, which, g).wait_send()
            grad_copy(side, g).wait_send()
        for which in range(4):
            out_copy(which, g).wait()
        return carry

    lax.fori_loop(0, groups, drain, 0)
    for copy in c1_copies + c2_copies + yg_copies:
        copy.wait_send()
    for part in range(parts):
        for k in range(1, Z):
            z_copy(k, part).wait_send()
            fg_copy(k, part).wait_send()
        for s in range(len(MID)):
            mg_copy(s, part).wait_send()


def per_device(queries, keys, values, cotangent, restrict_one, restrict_two):
    rows, width = queries.shape
    groups = width // PAIR
    parts = 2
    shape = jax.ShapeDtypeStruct((rows, width), BF16)
    hbm = pl.BlockSpec(memory_space=pl.ANY)
    vmem = pl.BlockSpec(memory_space=pltpu.VMEM)
    dma = pltpu.SemaphoreType.DMA
    mid = len(MID)
    scratch = [
        pltpu.VMEM((4, ROWS, width), BF16),
        pltpu.VMEM((2, groups, 2 * ROWS, PAIR), BF16),
        pltpu.VMEM((2, groups, 2 * ROWS, PAIR), BF16),
        pltpu.VMEM((2, groups, 2 * ROWS, PAIR), BF16),
        pltpu.VMEM((groups, 2 * ROWS, PAIR), F32),
        pltpu.VMEM((2, ROWS, width), BF16),
        pltpu.VMEM((16, width), BF16),
        pltpu.VMEM((mid, 16, width), BF16),
        pltpu.VMEM((16, width // 2), BF16),
        pltpu.VMEM((Y - 1, 16, width // 2), BF16),
        pltpu.VMEM((2, 16, width), BF16),
        pltpu.VMEM((mid, 16, width), BF16),
        pltpu.VMEM((mid, 16, width), BF16),
        pltpu.VMEM((Z - 1, 2, 16, width), BF16),
        pltpu.VMEM((Z - 1, 2, 16, width), BF16),
        pltpu.VMEM((Y - 1, 16, width // 2), BF16),
        pltpu.VMEM((Y - 1, 16, width // 2), BF16),
        pltpu.VMEM((16, ROWS), F32),
        pltpu.VMEM((16, width // 2), F32),
        pltpu.VMEM((2, 16, width), F32),
        pltpu.VMEM((COARSE, ROWS), F32),
        pltpu.VMEM((2 * ROWS, PAIR), BF16),
        pltpu.VMEM((2 * ROWS, PAIR), BF16),
        pltpu.VMEM((PAIR, PADDED), BF16),
        pltpu.VMEM((PAIR, PADDED), BF16),
        pltpu.VMEM((PAIR, ROWS), F32),
        pltpu.VMEM((2, KEYS, ROWS), F32),
        pltpu.VMEM((2, KEYS, ROWS), F32),
        pltpu.VMEM((PADDED, 2 * ROWS), BF16),
        pltpu.VMEM((PADDED, 2 * ROWS), BF16),
        pltpu.VMEM((PAIR, ROWS), F32),
        pltpu.VMEM((PAIR, ROWS), F32),
        pltpu.VMEM((4, groups, ROWS, PAIR), BF16),
        pltpu.VMEM((2, 16, width), F32),
        pltpu.VMEM((ROWS, 16), BF16),
        dma((4,)),
        dma((2, 2, groups)), dma((2, 2, groups)),
        dma((2, groups)), dma((2, groups)),
        dma((mid,)), dma((mid,)),
        dma((Y - 1,)), dma((Y - 1,)),
        dma((parts, Z - 1)), dma((parts, Z - 1)),
        dma((parts, mid)), dma((parts, mid)),
        dma((parts, Z - 1)), dma((parts, Z - 1)),
        dma((Y - 1,)), dma((Y - 1,)),
        dma((4, groups)),
    ]
    return pl.pallas_call(
        functools.partial(kernel, groups, parts),
        out_shape=[shape] * 4,
        in_specs=[hbm] * 4 + [vmem] * 2,
        out_specs=[hbm] * 4,
        scratch_shapes=scratch,
        compiler_params=pltpu.CompilerParams(
            collective_id=0, has_side_effects=True, vmem_limit_bytes=56 * 1024 * 1024
        ),
    )(queries, keys, values, cotangent, restrict_one, restrict_two)


def solution(mesh):
    rows = P(("prompt", "seq"), None)
    return jax.shard_map(
        per_device, mesh=mesh, in_specs=(rows, rows, rows, rows, P(), P()),
        out_specs=(rows, rows, rows, rows), check_vma=False,
    )
```

time: 450 us -> 99.8 us (0.22); the launches traced: 444 us -> 99.6 us
  waiting for transfers between devices: 121 us -> 0 us
  matrix products: 96 us -> 0 us
  Pallas kernels: 0 us -> 93.8 us
  local copies, waits for them, and re-layouts: 76.3 us -> 5.18 us
  blocking collectives: 63.7 us -> 0 us
  other arithmetic: 35.8 us -> 0 us
  starting transfers between devices: 34.5 us -> 0 us
  between operations: 16.1 us -> 0.65 us
    unnamed x2 -> x0, waiting for transfers between devices: 119 us -> none
    dot_general x52 -> x0, matrix products: 96 us -> none  [the longest x8 30.3 us: key_terms(): jnp.einsum('hqk,qhd->khd', weights, cotangent_group, preferred_element_ty...]
    pallas_call x0 -> x1, Pallas kernels: none -> 93.8 us  [per_device(): pl.pallas_call(functools.partial(kernel, groups, parts), out_shape=[shape...]
    all_gather x1 -> x0, blocking collectives: 63.7 us -> none  [per_device(): distant_keys = lax.all_gather(coarse_two, 'seq', axis=0, tiled=True)]
    ppermute x12 -> x0, starting transfers between devices: 34.5 us -> none  [the longest x10 28.6 us: from_behind(): return lax.ppermute(value, axis, pairs)]
    unnamed x200 -> x10, local copies, waits for them, and re-layouts: 37.5 us -> 5.18 us
    sub x8 -> x0, other arithmetic: 30.2 us -> none  [per_device(): raised = jnp.exp(scores - highest[:, :, None])]
    reshape x32 -> x0, local copies, waits for them, and re-layouts: 21.6 us -> none  [the longest x16 12.5 us: key_terms(): return (grad_key.reshape(key_count, -1), grad_value.reshape(key_count, -1))]
  transfers between devices with their start and end apart: 13 -> 0, of which waited for: 2 -> 0; matrix products, arithmetic and copies ran while one was open for 5% -> 0% of each run, Pallas kernels for 0% -> 0%
where the time goes in v1:
time: 99.8 us; the launch traced here: 99.6 us
  Pallas kernels  93.8 us (94%)
  local copies, waits for them, and re-layouts  5.18 us (5%)
    pallas_call x1, Pallas kernels, per_device(): pl.pallas_call(functools.partial(kernel, groups, parts), out_shape=[shape...  93.8 us
    unnamed x10, local copies, waits for them, and re-layouts  5.18 us

profile of v1, /device:TPU:2, one launch (start us, length us, event | category | flops | bytes accessed | tf_op | source)
XLA Modules:
  0.0 99.6 jit_solution(4385776195699205510)
XLA Ops:
  0.6 93.8 %shard_map.93 = (bf16[256,1024]{1,0:T(8,128)(2,1)}, bf16[256,1024]{1,0:T(8,128)(2,1)}, bf16[256,1024]{1,0:T(8,128)(2,1)}, bf16[256,1024]{1,0:T(8,128)(2,1)}) custom-call(bf16[256,1024]{1,0:T(8,128)(2,1)} %q_hbm.1, bf16[256,1024]{1,0:T(8,128)(2,1)} %k_hbm.1, bf16[256,1024]{1,0:T(8,128)(2,1)} %v_hbm.1, bf16[256,1024]{1,0:T(8,128)(2,1)} %do_hbm.1, ...), custom_call_target="tpu_custom_call" | custom-call | tf_op jit(solution)/shard_map/pallas_call | solution.py:462
  94.4 0.0 copy-start.2
  94.4 1.9 %copy.14 = bf16[256,1024]{1,0:T(8,128)(2,1)} copy(bf16[256,1024]{1,0:T(8,128)(2,1)} %get-tuple-element.8) | data formatting | bytes 1048576
  96.3 0.0 copy-done.2
  96.3 0.0 copy-start.1
  96.3 0.8 copy.15
  97.1 0.4 copy-done.1
  97.6 0.0 copy-start
  97.6 0.8 copy.16
  98.4 0.4 copy-done
  98.8 0.8 copy.17
Async XLA Ops:
  94.4 1.9 %copy-start.2 = (bf16[256,1024]{1,0:T(8,128)(2,1)S(1)}, bf16[256,1024]{1,0:T(8,128)(2,1)}, u32[]{:S(2)}) copy-start(bf16[256,1024]{1,0:T(8,128)(2,1)} %get-tuple-element.9) | copy-start | bytes 1572868
  96.3 1.2 %copy-start.1 = (bf16[256,1024]{1,0:T(8,128)(2,1)S(1)}, bf16[256,1024]{1,0:T(8,128)(2,1)}, u32[]{:S(2)}) copy-start(bf16[256,1024]{1,0:T(8,128)(2,1)} %get-tuple-element.10) | copy-start | bytes 1572868
  97.6 1.2 %copy-start = (bf16[256,1024]{1,0:T(8,128)(2,1)S(1)}, bf16[256,1024]{1,0:T(8,128)(2,1)}, u32[]{:S(2)}) copy-start(bf16[256,1024]{1,0:T(8,128)(2,1)} %get-tuple-element.11) | copy-start | bytes 1572868

commit v2 on v1

--- a/solution.py
+++ b/solution.py
@@ -45,14 +45,14 @@
 def kernel(
     groups, parts,
     q_hbm, k_hbm, v_hbm, do_hbm, r1_ref, r2_ref,
-    att_hbm, gq_hbm, gk_hbm, gv_hbm,
+    stage,
     own_in, near_kv, near_send, near_recv, own_grad, coarse,
     c1_send, c1_recv, c2_send, c2_recv, z_send, mg_send, mg_recv, fg_send, fg_recv, yg_send, yg_recv,
-    restrict, pack, gathered, bias, q_stack, do_stack, key_t, value_t, do_t, score, dots, prob, grad,
-    att_t, gq_t, stage, coarse_sum, restrict_t,
+    fg_own, restrict, pack, gathered, bias, q_stack, do_stack, key_t, value_t, do_t, score, dots, prob, grad,
+    att_t, gq_t, coarse_sum, restrict_t,
     load_sem, near_send_sem, near_recv_sem, grad_send_sem, grad_recv_sem,
     c1_send_sem, c1_recv_sem, c2_send_sem, c2_recv_sem, z_send_sem, z_recv_sem,
-    mg_send_sem, mg_recv_sem, fg_send_sem, fg_recv_sem, yg_send_sem, yg_recv_sem, out_sem,
+    mg_send_sem, mg_recv_sem, fg_send_sem, fg_recv_sem, yg_send_sem, yg_recv_sem,
 ):
     width = groups * PAIR
     half = width // 2
@@ -61,6 +61,7 @@
     me = lax.axis_index("seq")
     z = me // Y
     y = me % Y
+    way = 1 - 2 * (y // 2)
 
     def at_block(offset):
         return lax.rem(me + offset + BLOCKS, BLOCKS)
@@ -86,29 +87,6 @@
     ]
     for load in loads:
         load.start()
-
-    barrier = pltpu.get_barrier_semaphore()
-    partners = [at_block(o) for o in (-1, 1) + MID]
-    partners += [at_y(j) for j in range(1, Y)] + [at_z(k) for k in range(1, Z)]
-    for partner in partners:
-        pl.semaphore_signal(barrier, inc=1, device_id={"seq": partner}, device_id_type=MESH)
-    pl.semaphore_wait(barrier, len(partners))
-
-    def near_copy(side, which, g):
-        src = (k_hbm, v_hbm)[which].at[:, columns(g, PAIR)]
-        return remote(
-            src, near_kv.at[side, g, pl.ds(which * ROWS, ROWS)],
-            near_send_sem.at[side, which, g], near_recv_sem.at[side, which, g],
-            at_block(1 if side == 0 else -1),
-        )
-
-    def send_near(g, carry):
-        for side in range(2):
-            for which in range(2):
-                near_copy(side, which, g).start()
-        return carry
-
-    lax.fori_loop(0, groups, send_near, 0)
 
     restrict[...] = jnp.zeros_like(restrict)
     restrict[0:ONE, :] = r1_ref[...].astype(F32)
@@ -130,19 +108,7 @@
         return pack[...].astype(BF16)
 
     c2_send[...] = pack_rows(ONE)
-    c2_copies = [
-        remote(c2_send, c2_recv.at[j - 1], c2_send_sem.at[j - 1], c2_recv_sem.at[j - 1], at_y(j))
-        for j in range(1, Y)
-    ]
-    for copy in c2_copies:
-        copy.start()
     c1_send[...] = jnp.concatenate([coarse_k[0:ONE], coarse_v[0:ONE]], axis=0).astype(BF16)
-    c1_copies = [
-        remote(c1_send, c1_recv.at[s], c1_send_sem.at[s], c1_recv_sem.at[s], at_block(-o))
-        for s, o in enumerate(MID)
-    ]
-    for copy in c1_copies:
-        copy.start()
 
     row = lax.broadcasted_iota(jnp.int32, (COARSE, ROWS), 0)
     slot = row >> 3
@@ -150,7 +116,7 @@
     place = me + offset
     middle = jnp.where((place >= 0) & (place < BLOCKS), math.log(32.0), MASKED)
     far_row = row - MID_ROWS
-    far_z = (z - 1 - (far_row >> 4)) & (Z - 1)
+    far_z = (z - way * ((far_row >> 4) + 1)) & (Z - 1)
     far_y = (y - ((far_row >> 2) & 3)) & (Y - 1)
     distance = jnp.abs(far_z * Y + far_y - me)
     far = jnp.where(distance >= 4, math.log(64.0), MASKED)
@@ -161,6 +127,43 @@
         coarse[which, COARSE:ROWS, :] = jnp.zeros((ROWS - COARSE, width), BF16)
     prob[KEYS:PADDED, :] = jnp.zeros((PADDED - KEYS, 2 * ROWS), BF16)
     grad[KEYS:PADDED, :] = jnp.zeros((PADDED - KEYS, 2 * ROWS), BF16)
+
+    barrier = pltpu.get_barrier_semaphore()
+    partners = [at_block(o) for o in (-1, 1) + MID]
+    partners += [at_y(j) for j in range(1, Y)] + [at_z(-1), at_z(1)]
+    for partner in partners:
+        pl.semaphore_signal(barrier, inc=1, device_id={"seq": partner}, device_id_type=MESH)
+    pl.semaphore_wait(barrier, len(partners))
+
+    c2_copies = [
+        remote(c2_send, c2_recv.at[j - 1], c2_send_sem.at[j - 1], c2_recv_sem.at[j - 1], at_y(j))
+        for j in range(1, Y)
+    ]
+    for copy in c2_copies:
+        copy.start()
+    c1_copies = [
+        remote(c1_send, c1_recv.at[s], c1_send_sem.at[s], c1_recv_sem.at[s], at_block(-o))
+        for s, o in enumerate(MID)
+    ]
+    for copy in c1_copies:
+        copy.start()
+
+
+    def near_copy(side, which, g):
+        src = (k_hbm, v_hbm)[which].at[:, columns(g, PAIR)]
+        return remote(
+            src, near_kv.at[side, g, pl.ds(which * ROWS, ROWS)],
+            near_send_sem.at[side, which, g], near_recv_sem.at[side, which, g],
+            at_block(1 if side == 0 else -1),
+        )
+
+    def send_near(g, carry):
+        for side in range(2):
+            for which in range(2):
+                near_copy(side, which, g).start()
+        return carry
+
+    lax.fori_loop(0, groups, send_near, 0)
 
     for j in range(Y):
         if j == 0:
@@ -175,17 +178,19 @@
                 gathered[which, TWO * j:TWO * (j + 1), side * half:(side + 1) * half] = pack[first:first + TWO, :]
     z_send[...] = gathered[...].astype(BF16)
 
+    def far_slot(k):
+        return pl.ds(MID_ROWS + (k - 1) * Y * TWO, Y * TWO)
+
     def z_copy(k, part):
         cols = columns(part, part_width)
+        src = z_send.at[:, :, cols] if k == 1 else coarse.at[:, far_slot(k - 1), cols]
         return remote(
-            z_send.at[:, :, cols],
-            coarse.at[:, pl.ds(MID_ROWS + (k - 1) * Y * TWO, Y * TWO), cols],
-            z_send_sem.at[part, k - 1], z_recv_sem.at[part, k - 1], at_z(k),
+            src, coarse.at[:, far_slot(k), cols],
+            z_send_sem.at[part, k - 1], z_recv_sem.at[part, k - 1], at_z(way),
         )
 
     for part in range(parts):
-        for k in range(1, Z):
-            z_copy(k, part).start()
+        z_copy(1, part).start()
 
     for copy in c1_copies:
         copy.wait_recv()
@@ -194,6 +199,11 @@
         coarse[which, 0:MID_ROWS, :] = jnp.concatenate(rows, axis=0).astype(BF16)
     loads[2].wait()
     loads[3].wait()
+    for k in range(1, Z):
+        for part in range(parts):
+            z_copy(k, part).wait_recv()
+            if k < Z - 1:
+                z_copy(k + 1, part).start()
 
     def grad_copy(side, g):
         return remote(
@@ -209,25 +219,31 @@
             mg_send_sem.at[part, s], mg_recv_sem.at[part, s], at_block(MID[s]),
         )
 
-    def fg_copy(k, part):
-        cols = columns(part, part_width)
+    def fg_copy(t, g):
+        cols = columns(g, PAIR)
         return remote(
-            fg_send.at[k - 1, :, :, cols], fg_recv.at[k - 1, :, :, cols],
-            fg_send_sem.at[part, k - 1], fg_recv_sem.at[part, k - 1], at_z(-k),
+            fg_send.at[t, :, :, cols], fg_recv.at[t, :, :, cols],
+            fg_send_sem.at[t, g], fg_recv_sem.at[t, g], at_z(way),
         )
 
-    def out_copy(which, g):
-        out = (att_hbm, gq_hbm, gk_hbm, gv_hbm)[which]
-        return pltpu.make_async_copy(stage.at[which, g], out.at[:, columns(g, PAIR)], out_sem.at[which, g])
+    def ring_step(t, g):
+        cols = columns(g, PAIR)
+        total = fg_own[t, :, :, cols]
+        if t > 0:
+            fg_copy(t - 1, g).wait_recv()
+            total = total + fg_recv[t - 1, :, :, cols].astype(F32)
+        fg_send[t, :, :, cols] = total.astype(BF16)
+        fg_copy(t, g).start()
+
+    def ring_steps(turn):
+        for t in range(1, Z - 1):
+            @pl.when((turn - t >= 0) & (turn - t < groups))
+            def _(t=t):
+                ring_step(t, turn - t)
 
     def pair(g, carry):
         cols = columns(g, PAIR)
         part = g // part_groups
-
-        @pl.when(g % part_groups == 0)
-        def _():
-            for k in range(1, Z):
-                z_copy(k, part).wait_recv()
 
         for side in range(2):
             for which in range(2):
@@ -293,8 +309,6 @@
             gq_t[head, :] = dot(key_t[head, :], grad[:, lanes], 1, 0) * (1.0 / math.sqrt(HEAD_DIM))
         stage[0, g] = att_t[...].T.astype(BF16)
         stage[1, g] = gq_t[...].T.astype(BF16)
-        out_copy(0, g).start()
-        out_copy(1, g).start()
 
         def key_grads(first, n):
             return (
@@ -316,13 +330,13 @@
             mg_send[s, :, cols] = both.astype(BF16)
         for k in range(1, Z):
             first = MID_ROWS + (k - 1) * Y * TWO
-            fg_send[k - 1, 0, :, cols] = dk[first:first + Y * TWO].astype(BF16)
-            fg_send[k - 1, 1, :, cols] = dv[first:first + Y * TWO].astype(BF16)
+            fg_own[k - 1, 0, :, cols] = dk[first:first + Y * TWO]
+            fg_own[k - 1, 1, :, cols] = dv[first:first + Y * TWO]
+        ring_step(0, g)
+        ring_steps(g)
 
         @pl.when(g % part_groups == part_groups - 1)
         def _():
-            for k in range(1, Z):
-                fg_copy(k, part).start()
             for s in range(len(MID)):
                 mg_copy(s, part).start()
 
@@ -330,14 +344,28 @@
 
     lax.fori_loop(0, groups, pair, 0)
 
-    for part in range(parts):
-        for k in range(1, Z):
-            fg_copy(k, part).wait_recv()
+    def add_near(g):
+        for side in range(2):
+            grad_copy(side, g).wait_recv()
+        own_grad[g] = own_grad[g] + near_recv[0, g].astype(F32) + near_recv[1, g].astype(F32)
+
+    def tail(turn, carry):
+        ring_steps(turn)
+        add_near(turn - groups)
+        return carry
+
+    turns = min(groups, Z - 2)
+    lax.fori_loop(groups, groups + turns, tail, 0)
+    for turn in range(groups + turns, groups + Z - 2):
+        ring_steps(jnp.int32(turn))
+
+    def far_arrival(g, carry):
+        fg_copy(Z - 2, g).wait_recv()
+        return carry
+
+    lax.fori_loop(0, groups, far_arrival, 0)
     for which in range(2):
-        total = fg_recv[0, which].astype(F32)
-        for k in range(2, Z):
-            total = total + fg_recv[k - 1, which].astype(F32)
-        gathered[which] = total
+        gathered[which] = fg_recv[Z - 2, which].astype(F32)
     yg_copies = [
         remote(yg_send.at[j - 1], yg_recv.at[j - 1], yg_send_sem.at[j - 1], yg_recv_sem.at[j - 1], at_y(-j))
         for j in range(1, Y)
@@ -366,19 +394,18 @@
                     coarse_sum[which, ONE:ONE + TWO, cols] + pack[first:first + TWO, :]
                 )
 
+    for g in range(turns, groups):
+        add_near(g)
+
     def finish(g, carry):
         cols = columns(g, PAIR)
-        for side in range(2):
-            grad_copy(side, g).wait_recv()
         for which in range(2):
             rows = slice(which * ROWS, (which + 1) * ROWS)
             wide = coarse_sum[which, :, cols]
             high = wide.astype(BF16)
             low = (wide - high.astype(F32)).astype(BF16)
             total = own_grad[g, rows, :] + dot(restrict_t[...], high, 1, 0) + dot(restrict_t[...], low, 1, 0)
-            total = total + near_recv[0, g, rows, :].astype(F32) + near_recv[1, g, rows, :].astype(F32)
             stage[2 + which, g] = total.astype(BF16)
-            out_copy(2 + which, g).start()
         return carry
 
     lax.fori_loop(0, groups, finish, 0)
@@ -388,8 +415,8 @@
             for which in range(2):
                 near_copy(side, which, g).wait_send()
             grad_copy(side, g).wait_send()
-        for which in range(4):
-            out_copy(which, g).wait()
+        for t in range(Z - 1):
+            fg_copy(t, g).wait_send()
         return carry
 
     lax.fori_loop(0, groups, drain, 0)
@@ -398,9 +425,20 @@
     for part in range(parts):
         for k in range(1, Z):
             z_copy(k, part).wait_send()
-            fg_copy(k, part).wait_send()
         for s in range(len(MID)):
             mg_copy(s, part).wait_send()
+
+
+def write_out(groups, stage, att, gq, gk, gv, sem):
+    copies = [
+        pltpu.make_async_copy(stage.at[i, g], out.at[:, pl.ds(g * PAIR, PAIR)], sem.at[i, g])
+        for i, out in enumerate((att, gq, gk, gv))
+        for g in range(groups)
+    ]
+    for copy in copies:
+        copy.start()
+    for copy in copies:
+        copy.wait()
 
 
 def per_device(queries, keys, values, cotangent, restrict_one, restrict_two):
@@ -430,6 +468,7 @@
         pltpu.VMEM((Z - 1, 2, 16, width), BF16),
         pltpu.VMEM((Y - 1, 16, width // 2), BF16),
         pltpu.VMEM((Y - 1, 16, width // 2), BF16),
+        pltpu.VMEM((Z - 1, 2, 16, width), F32),
         pltpu.VMEM((16, ROWS), F32),
         pltpu.VMEM((16, width // 2), F32),
         pltpu.VMEM((2, 16, width), F32),
@@ -445,7 +484,6 @@
         pltpu.VMEM((PADDED, 2 * ROWS), BF16),
         pltpu.VMEM((PAIR, ROWS), F32),
         pltpu.VMEM((PAIR, ROWS), F32),
-        pltpu.VMEM((4, groups, ROWS, PAIR), BF16),
         pltpu.VMEM((2, 16, width), F32),
         pltpu.VMEM((ROWS, 16), BF16),
         dma((4,)),
@@ -455,20 +493,26 @@
         dma((Y - 1,)), dma((Y - 1,)),
         dma((parts, Z - 1)), dma((parts, Z - 1)),
         dma((parts, mid)), dma((parts, mid)),
-        dma((parts, Z - 1)), dma((parts, Z - 1)),
+        dma((Z - 1, groups)), dma((Z - 1, groups)),
         dma((Y - 1,)), dma((Y - 1,)),
-        dma((4, groups)),
     ]
-    return pl.pallas_call(
+    stage = pl.pallas_call(
         functools.partial(kernel, groups, parts),
-        out_shape=[shape] * 4,
+        out_shape=pltpu.VMEM((4, groups, ROWS, PAIR), BF16),
         in_specs=[hbm] * 4 + [vmem] * 2,
-        out_specs=[hbm] * 4,
+        out_specs=vmem,
         scratch_shapes=scratch,
         compiler_params=pltpu.CompilerParams(
             collective_id=0, has_side_effects=True, vmem_limit_bytes=56 * 1024 * 1024
         ),
     )(queries, keys, values, cotangent, restrict_one, restrict_two)
+    return pl.pallas_call(
+        functools.partial(write_out, groups),
+        out_shape=[shape] * 4,
+        in_specs=[vmem],
+        out_specs=[hbm] * 4,
+        scratch_shapes=[dma((4, groups))],
+    )(stage)
 
 
 def solution(mesh):

time: 99.8 us -> 117 us (1.17)
  Pallas kernels: 93.8 us -> 115 us
  local copies, waits for them, and re-layouts: 5.18 us -> 1.34 us
    pallas_call x1 -> x2, Pallas kernels: 93.8 us -> 115 us  [the longest x1 112 us: per_device(): pl.pallas_call(functools.partial(kernel, groups, parts), out_shape=pltpu....]
    unnamed x10 -> x2, local copies, waits for them, and re-layouts: 5.18 us -> 1.34 us
where the time goes in v2:
time: 117 us
  Pallas kernels  115 us (98%)
  local copies, waits for them, and re-layouts  1.34 us (1%)
    pallas_call x1, Pallas kernels, per_device(): pl.pallas_call(functools.partial(kernel, groups, parts), out_shape=pltpu....  112 us
    pallas_call x1, Pallas kernels, per_device(): pl.pallas_call(functools.partial(write_out, groups), out_shape=[shape] *...  3.16 us

profile of v2, /device:TPU:2, one launch (start us, length us, event | category | flops | bytes accessed | tf_op | source)
XLA Modules:
  0.0 117.2 jit_solution(6117332839751946231)
XLA Ops:
  0.6 112.1 %shard_map.93.stage = bf16[4,8,256,128]{3,2,1,0:T(8,128)(2,1)S(1)} custom-call(bf16[256,1024]{1,0:T(8,128)(2,1)} %q_hbm.1, bf16[256,1024]{1,0:T(8,128)(2,1)} %k_hbm.1, bf16[256,1024]{1,0:T(8,128)(2,1)} %v_hbm.1, bf16[256,1024]{1,0:T(8,128)(2,1)} %do_hbm.1, bf16[8,256]{1,0:T(8,128)(2,1)} %r1_ref.1, bf16[4,256]{1,0:T(4,128)(2,1)} %r2_ref.1), custom_call_target="tpu_custom_call" | custom-call | tf_op jit(solution)/shard_map/pallas_call | solution.py:499
  112.7 0.0 copy-start
  112.8 1.3 %copy-done = bf16[4,8,256,128]{3,2,1,0:T(8,128)(2,1)} copy-done((bf16[4,8,256,128]{3,2,1,0:T(8,128)(2,1)}, bf16[4,8,256,128]{3,2,1,0:T(8,128)(2,1)S(1)}, u32[]{:S(2)}) %copy-start) | copy-done | bytes 2097176
  114.1 3.2 %shard_map.94 = (bf16[256,1024]{1,0:T(8,128)(2,1)}, bf16[256,1024]{1,0:T(8,128)(2,1)}, bf16[256,1024]{1,0:T(8,128)(2,1)}, bf16[256,1024]{1,0:T(8,128)(2,1)}) custom-call(bf16[4,8,256,128]{3,2,1,0:T(8,128)(2,1)} %copy-done), custom_call_target="tpu_custom_call" | custom-call | tf_op jit(solution)/shard_map/pallas_call | solution.py:509
Async XLA Ops:
  112.7 1.3 %copy-start = (bf16[4,8,256,128]{3,2,1,0:T(8,128)(2,1)}, bf16[4,8,256,128]{3,2,1,0:T(8,128)(2,1)S(1)}, u32[]{:S(2)}) copy-start(bf16[4,8,256,128]{3,2,1,0:T(8,128)(2,1)S(1)} %shard_map.93.stage) | copy-start | bytes 6291460

commit v3 on v1

--- a/solution.py
+++ b/solution.py
@@ -17,6 +17,8 @@
 ONE = 8
 TWO = 4
 MID = (-3, -2, 2, 3)
+FG_STEPS = (3, -1, 3, 2, 1)
+Z_STEPS = {1: 1, 2: 2, 3: 3, 4: 1, 5: 2, 6: 3, 7: -1}
 MID_ROWS = len(MID) * ONE
 FAR_ROWS = (Z - 1) * Y * TWO
 COARSE = MID_ROWS + FAR_ROWS
@@ -45,14 +47,14 @@
 def kernel(
     groups, parts,
     q_hbm, k_hbm, v_hbm, do_hbm, r1_ref, r2_ref,
-    att_hbm, gq_hbm, gk_hbm, gv_hbm,
+    stage,
     own_in, near_kv, near_send, near_recv, own_grad, coarse,
     c1_send, c1_recv, c2_send, c2_recv, z_send, mg_send, mg_recv, fg_send, fg_recv, yg_send, yg_recv,
-    restrict, pack, gathered, bias, q_stack, do_stack, key_t, value_t, do_t, score, dots, prob, grad,
-    att_t, gq_t, stage, coarse_sum, restrict_t,
+    fg_own, restrict, pack, gathered, bias, q_stack, do_stack, key_t, value_t, do_t, score, dots, prob, grad,
+    att_t, gq_t, coarse_sum, restrict_t,
     load_sem, near_send_sem, near_recv_sem, grad_send_sem, grad_recv_sem,
     c1_send_sem, c1_recv_sem, c2_send_sem, c2_recv_sem, z_send_sem, z_recv_sem,
-    mg_send_sem, mg_recv_sem, fg_send_sem, fg_recv_sem, yg_send_sem, yg_recv_sem, out_sem,
+    mg_send_sem, mg_recv_sem, fg_send_sem, fg_recv_sem, yg_send_sem, yg_recv_sem, go_sem,
 ):
     width = groups * PAIR
     half = width // 2
@@ -61,6 +63,7 @@
     me = lax.axis_index("seq")
     z = me // Y
     y = me % Y
+    way = 1 - 2 * (y // 2)
 
     def at_block(offset):
         return lax.rem(me + offset + BLOCKS, BLOCKS)
@@ -89,7 +92,7 @@
 
     barrier = pltpu.get_barrier_semaphore()
     partners = [at_block(o) for o in (-1, 1) + MID]
-    partners += [at_y(j) for j in range(1, Y)] + [at_z(k) for k in range(1, Z)]
+    partners += [at_y(j) for j in range(1, Y)] + [at_z(k) for k in (-3, -2, -1, 1, 2, 3)]
     for partner in partners:
         pl.semaphore_signal(barrier, inc=1, device_id={"seq": partner}, device_id_type=MESH)
     pl.semaphore_wait(barrier, len(partners))
@@ -102,13 +105,13 @@
             at_block(1 if side == 0 else -1),
         )
 
-    def send_near(g, carry):
-        for side in range(2):
-            for which in range(2):
-                near_copy(side, which, g).start()
+    def send_near(side, g, carry):
+        for which in range(2):
+            near_copy(side, which, g).start()
         return carry
 
-    lax.fori_loop(0, groups, send_near, 0)
+    for side in range(2):
+        send_near(side, 0, 0)
 
     restrict[...] = jnp.zeros_like(restrict)
     restrict[0:ONE, :] = r1_ref[...].astype(F32)
@@ -130,13 +133,14 @@
         return pack[...].astype(BF16)
 
     c2_send[...] = pack_rows(ONE)
+    c1_send[...] = jnp.concatenate([coarse_k[0:ONE], coarse_v[0:ONE]], axis=0).astype(BF16)
+
     c2_copies = [
         remote(c2_send, c2_recv.at[j - 1], c2_send_sem.at[j - 1], c2_recv_sem.at[j - 1], at_y(j))
         for j in range(1, Y)
     ]
     for copy in c2_copies:
         copy.start()
-    c1_send[...] = jnp.concatenate([coarse_k[0:ONE], coarse_v[0:ONE]], axis=0).astype(BF16)
     c1_copies = [
         remote(c1_send, c1_recv.at[s], c1_send_sem.at[s], c1_recv_sem.at[s], at_block(-o))
         for s, o in enumerate(MID)
@@ -144,13 +148,19 @@
     for copy in c1_copies:
         copy.start()
 
+    wraps = (y == Y - 1, y == 0)
+    for side in range(2):
+        @pl.when(jnp.logical_not(wraps[side]))
+        def _(side=side):
+            lax.fori_loop(1, groups, functools.partial(send_near, side), 0)
+
     row = lax.broadcasted_iota(jnp.int32, (COARSE, ROWS), 0)
     slot = row >> 3
     offset = jnp.where(slot == 0, -3, jnp.where(slot == 1, -2, jnp.where(slot == 2, 2, 3)))
     place = me + offset
     middle = jnp.where((place >= 0) & (place < BLOCKS), math.log(32.0), MASKED)
     far_row = row - MID_ROWS
-    far_z = (z - 1 - (far_row >> 4)) & (Z - 1)
+    far_z = (z - way * ((far_row >> 4) + 1)) & (Z - 1)
     far_y = (y - ((far_row >> 2) & 3)) & (Y - 1)
     distance = jnp.abs(far_z * Y + far_y - me)
     far = jnp.where(distance >= 4, math.log(64.0), MASKED)
@@ -162,11 +172,17 @@
     prob[KEYS:PADDED, :] = jnp.zeros((PADDED - KEYS, 2 * ROWS), BF16)
     grad[KEYS:PADDED, :] = jnp.zeros((PADDED - KEYS, 2 * ROWS), BF16)
 
+    for copy in c2_copies + c1_copies:
+        copy.wait_recv()
+    for side in range(2):
+        pl.semaphore_signal(
+            go_sem.at[side], inc=1, device_id={"seq": at_block(-1 if side == 0 else 1)}, device_id_type=MESH
+        )
+
     for j in range(Y):
         if j == 0:
             block = c2_send[...]
         else:
-            c2_copies[j - 1].wait_recv()
             block = c2_recv[j - 1]
         pack[...] = block.astype(F32)
         for which in range(2):
@@ -175,25 +191,40 @@
                 gathered[which, TWO * j:TWO * (j + 1), side * half:(side + 1) * half] = pack[first:first + TWO, :]
     z_send[...] = gathered[...].astype(BF16)
 
+    def far_slot(k):
+        return pl.ds(MID_ROWS + (k - 1) * Y * TWO, Y * TWO)
+
     def z_copy(k, part):
         cols = columns(part, part_width)
+        src = coarse.at[:, far_slot(3), cols] if k in (4, 5, 6) else z_send.at[:, :, cols]
         return remote(
-            z_send.at[:, :, cols],
-            coarse.at[:, pl.ds(MID_ROWS + (k - 1) * Y * TWO, Y * TWO), cols],
-            z_send_sem.at[part, k - 1], z_recv_sem.at[part, k - 1], at_z(k),
-        )
-
-    for part in range(parts):
-        for k in range(1, Z):
+            src, coarse.at[:, far_slot(k), cols],
+            z_send_sem.at[part, k - 1], z_recv_sem.at[part, k - 1], at_z(way * Z_STEPS[k]),
+        )
+
+    def z_own(part):
+        for k in (3, 2, 1, 7):
             z_copy(k, part).start()
 
-    for copy in c1_copies:
-        copy.wait_recv()
+    z_own(0)
+    z_own(1)
+    for side in range(2):
+        @pl.when(wraps[side])
+        def _(side=side):
+            pl.semaphore_wait(go_sem.at[side], 1)
+            lax.fori_loop(1, groups, functools.partial(send_near, side), 0)
+
     for which in range(2):
         rows = [c1_recv[s].astype(F32)[which * ONE:(which + 1) * ONE] for s in range(len(MID))]
         coarse[which, 0:MID_ROWS, :] = jnp.concatenate(rows, axis=0).astype(BF16)
     loads[2].wait()
     loads[3].wait()
+    for part in range(parts):
+        z_copy(3, part).wait_recv()
+        for k in (6, 5, 4):
+            z_copy(k, part).start()
+        if part + 2 < parts:
+            z_own(part + 2)
 
     def grad_copy(side, g):
         return remote(
@@ -209,16 +240,28 @@
             mg_send_sem.at[part, s], mg_recv_sem.at[part, s], at_block(MID[s]),
         )
 
-    def fg_copy(k, part):
-        cols = columns(part, part_width)
+    def fg_copy(i, g):
+        cols = columns(g, PAIR)
+        slots = pl.ds(0, 3) if i == 0 else pl.ds(2 + i, 1)
         return remote(
-            fg_send.at[k - 1, :, :, cols], fg_recv.at[k - 1, :, :, cols],
-            fg_send_sem.at[part, k - 1], fg_recv_sem.at[part, k - 1], at_z(-k),
-        )
-
-    def out_copy(which, g):
-        out = (att_hbm, gq_hbm, gk_hbm, gv_hbm)[which]
-        return pltpu.make_async_copy(stage.at[which, g], out.at[:, columns(g, PAIR)], out_sem.at[which, g])
+            fg_send.at[slots, :, :, cols], fg_recv.at[slots, :, :, cols],
+            fg_send_sem.at[i, g], fg_recv_sem.at[i, g], at_z(way * FG_STEPS[i]),
+        )
+
+    def sum_first(g):
+        cols = columns(g, PAIR)
+        for i, k in enumerate((2, 3, 4, 1)):
+            fg_send[i, :, :, cols] = fg_own[k - 1, :, :, cols].astype(BF16)
+        for i in range(2):
+            fg_copy(i, g).start()
+
+    def sum_second(g):
+        cols = columns(g, PAIR)
+        fg_copy(0, g).wait_recv()
+        for i in range(3):
+            total = fg_own[4 + i, :, :, cols] + fg_recv[i, :, :, cols].astype(F32)
+            fg_send[4 + i, :, :, cols] = total.astype(BF16)
+            fg_copy(2 + i, g).start()
 
     def pair(g, carry):
         cols = columns(g, PAIR)
@@ -226,7 +269,7 @@
 
         @pl.when(g % part_groups == 0)
         def _():
-            for k in range(1, Z):
+            for k in (1, 2, 4, 5, 6, 7):
                 z_copy(k, part).wait_recv()
 
         for side in range(2):
@@ -291,10 +334,8 @@
                 p = score[h, c:c + CHUNK, :] * inverse
                 grad[c:c + CHUNK, lanes] = (p * (dots[h, c:c + CHUNK, :] - delta)).astype(BF16)
             gq_t[head, :] = dot(key_t[head, :], grad[:, lanes], 1, 0) * (1.0 / math.sqrt(HEAD_DIM))
-        stage[0, g] = att_t[...].T.astype(BF16)
-        stage[1, g] = gq_t[...].T.astype(BF16)
-        out_copy(0, g).start()
-        out_copy(1, g).start()
+        stage[0, :, cols] = att_t[...].T.astype(BF16)
+        stage[1, :, cols] = gq_t[...].T.astype(BF16)
 
         def key_grads(first, n):
             return (
@@ -316,13 +357,17 @@
             mg_send[s, :, cols] = both.astype(BF16)
         for k in range(1, Z):
             first = MID_ROWS + (k - 1) * Y * TWO
-            fg_send[k - 1, 0, :, cols] = dk[first:first + Y * TWO].astype(BF16)
-            fg_send[k - 1, 1, :, cols] = dv[first:first + Y * TWO].astype(BF16)
+            fg_own[k - 1, 0, :, cols] = dk[first:first + Y * TWO]
+            fg_own[k - 1, 1, :, cols] = dv[first:first + Y * TWO]
+        sum_first(g)
+
+        @pl.when(g > 0)
+        def _():
+            sum_second(g - 1)
+
 
         @pl.when(g % part_groups == part_groups - 1)
         def _():
-            for k in range(1, Z):
-                fg_copy(k, part).start()
             for s in range(len(MID)):
                 mg_copy(s, part).start()
 
@@ -330,13 +375,25 @@
 
     lax.fori_loop(0, groups, pair, 0)
 
-    for part in range(parts):
-        for k in range(1, Z):
-            fg_copy(k, part).wait_recv()
+    def add_near(g):
+        for side in range(2):
+            grad_copy(side, g).wait_recv()
+        own_grad[g] = own_grad[g] + near_recv[0, g].astype(F32) + near_recv[1, g].astype(F32)
+
+    def far_arrival(g, carry):
+        for i in range(1, 5):
+            fg_copy(i, g).wait_recv()
+        return carry
+
+    sum_second(groups - 1)
+    early = groups - 2
+    for g in range(early):
+        add_near(g)
+    lax.fori_loop(0, groups, far_arrival, 0)
     for which in range(2):
-        total = fg_recv[0, which].astype(F32)
-        for k in range(2, Z):
-            total = total + fg_recv[k - 1, which].astype(F32)
+        total = fg_recv[3, which].astype(F32)
+        for i in range(4, 7):
+            total = total + fg_recv[i, which].astype(F32)
         gathered[which] = total
     yg_copies = [
         remote(yg_send.at[j - 1], yg_recv.at[j - 1], yg_send_sem.at[j - 1], yg_recv_sem.at[j - 1], at_y(-j))
@@ -366,19 +423,18 @@
                     coarse_sum[which, ONE:ONE + TWO, cols] + pack[first:first + TWO, :]
                 )
 
+    for g in range(early, groups):
+        add_near(g)
+
     def finish(g, carry):
         cols = columns(g, PAIR)
-        for side in range(2):
-            grad_copy(side, g).wait_recv()
         for which in range(2):
             rows = slice(which * ROWS, (which + 1) * ROWS)
             wide = coarse_sum[which, :, cols]
             high = wide.astype(BF16)
             low = (wide - high.astype(F32)).astype(BF16)
             total = own_grad[g, rows, :] + dot(restrict_t[...], high, 1, 0) + dot(restrict_t[...], low, 1, 0)
-            total = total + near_recv[0, g, rows, :].astype(F32) + near_recv[1, g, rows, :].astype(F32)
-            stage[2 + which, g] = total.astype(BF16)
-            out_copy(2 + which, g).start()
+            stage[2 + which, :, cols] = total.astype(BF16)
         return carry
 
     lax.fori_loop(0, groups, finish, 0)
@@ -388,25 +444,39 @@
             for which in range(2):
                 near_copy(side, which, g).wait_send()
             grad_copy(side, g).wait_send()
-        for which in range(4):
-            out_copy(which, g).wait()
+        for i in range(5):
+            fg_copy(i, g).wait_send()
         return carry
 
     lax.fori_loop(0, groups, drain, 0)
+    for side in range(2):
+        @pl.when(jnp.logical_not(wraps[side]))
+        def _(side=side):
+            pl.semaphore_wait(go_sem.at[side], 1)
+
     for copy in c1_copies + c2_copies + yg_copies:
         copy.wait_send()
     for part in range(parts):
         for k in range(1, Z):
             z_copy(k, part).wait_send()
-            fg_copy(k, part).wait_send()
         for s in range(len(MID)):
             mg_copy(s, part).wait_send()
+
+
+def write_out(stage, att, gq, gk, gv, sem):
+    copies = [
+        pltpu.make_async_copy(stage.at[i], out, sem.at[i]) for i, out in enumerate((att, gq, gk, gv))
+    ]
+    for copy in copies:
+        copy.start()
+    for copy in copies:
+        copy.wait()
 
 
 def per_device(queries, keys, values, cotangent, restrict_one, restrict_two):
     rows, width = queries.shape
     groups = width // PAIR
-    parts = 2
+    parts = 4 if groups % 4 == 0 else 2
     shape = jax.ShapeDtypeStruct((rows, width), BF16)
     hbm = pl.BlockSpec(memory_space=pl.ANY)
     vmem = pl.BlockSpec(memory_space=pltpu.VMEM)
@@ -430,6 +500,7 @@
         pltpu.VMEM((Z - 1, 2, 16, width), BF16),
         pltpu.VMEM((Y - 1, 16, width // 2), BF16),
         pltpu.VMEM((Y - 1, 16, width // 2), BF16),
+        pltpu.VMEM((Z - 1, 2, 16, width), F32),
         pltpu.VMEM((16, ROWS), F32),
         pltpu.VMEM((16, width // 2), F32),
         pltpu.VMEM((2, 16, width), F32),
@@ -445,7 +516,6 @@
         pltpu.VMEM((PADDED, 2 * ROWS), BF16),
         pltpu.VMEM((PAIR, ROWS), F32),
         pltpu.VMEM((PAIR, ROWS), F32),
-        pltpu.VMEM((4, groups, ROWS, PAIR), BF16),
         pltpu.VMEM((2, 16, width), F32),
         pltpu.VMEM((ROWS, 16), BF16),
         dma((4,)),
@@ -455,20 +525,27 @@
         dma((Y - 1,)), dma((Y - 1,)),
         dma((parts, Z - 1)), dma((parts, Z - 1)),
         dma((parts, mid)), dma((parts, mid)),
-        dma((parts, Z - 1)), dma((parts, Z - 1)),
+        dma((5, groups)), dma((5, groups)),
         dma((Y - 1,)), dma((Y - 1,)),
-        dma((4, groups)),
+        pltpu.SemaphoreType.REGULAR((2,)),
     ]
-    return pl.pallas_call(
+    stage = pl.pallas_call(
         functools.partial(kernel, groups, parts),
-        out_shape=[shape] * 4,
+        out_shape=pltpu.VMEM((4, ROWS, width), BF16),
         in_specs=[hbm] * 4 + [vmem] * 2,
-        out_specs=[hbm] * 4,
+        out_specs=vmem,
         scratch_shapes=scratch,
         compiler_params=pltpu.CompilerParams(
             collective_id=0, has_side_effects=True, vmem_limit_bytes=56 * 1024 * 1024
         ),
     )(queries, keys, values, cotangent, restrict_one, restrict_two)
+    return pl.pallas_call(
+        write_out,
+        out_shape=[shape] * 4,
+        in_specs=[vmem],
+        out_specs=[hbm] * 4,
+        scratch_shapes=[dma((4,))],
+    )(stage)
 
 
 def solution(mesh):

time: 99.8 us -> 84.6 us (0.85)
  Pallas kernels: 93.8 us -> 82.4 us
  local copies, waits for them, and re-layouts: 5.18 us -> 1.34 us
    pallas_call x1 -> x2, Pallas kernels: 93.8 us -> 82.4 us  [the longest x1 79.4 us: per_device(): pl.pallas_call(functools.partial(kernel, groups, parts), out_shape=pltpu....]
    unnamed x10 -> x2, local copies, waits for them, and re-layouts: 5.18 us -> 1.34 us
where the time goes in v3:
time: 84.6 us; the launch traced here: 84.3 us
  Pallas kernels  82.4 us (97%)
  local copies, waits for them, and re-layouts  1.34 us (2%)
    pallas_call x1, Pallas kernels, per_device(): pl.pallas_call(functools.partial(kernel, groups, parts), out_shape=pltpu....  79.4 us
    pallas_call x1, Pallas kernels, per_device(): pl.pallas_call(write_out, out_shape=[shape] * 4, in_specs=[vmem], out_spe...  2.93 us

profile of v3, /device:TPU:2, one launch (start us, length us, event | category | flops | bytes accessed | tf_op | source)
XLA Modules:
  0.0 84.3 jit_solution(5881982205606759765)
XLA Ops:
  0.6 79.4 %shard_map.93.stage = bf16[4,256,1024]{2,1,0:T(8,128)(2,1)S(1)} custom-call(bf16[256,1024]{1,0:T(8,128)(2,1)} %q_hbm.1, bf16[256,1024]{1,0:T(8,128)(2,1)} %k_hbm.1, bf16[256,1024]{1,0:T(8,128)(2,1)} %v_hbm.1, bf16[256,1024]{1,0:T(8,128)(2,1)} %do_hbm.1, bf16[8,256]{1,0:T(8,128)(2,1)} %r1_ref.1, bf16[4,256]{1,0:T(4,128)(2,1)} %r2_ref.1), custom_call_target="tpu_custom_call" | custom-call | tf_op jit(solution)/shard_map/pallas_call | solution.py:532
  80.1 0.0 copy-start
  80.1 1.3 %copy-done = bf16[4,256,1024]{2,1,0:T(8,128)(2,1)} copy-done((bf16[4,256,1024]{2,1,0:T(8,128)(2,1)}, bf16[4,256,1024]{2,1,0:T(8,128)(2,1)S(1)}, u32[]{:S(2)}) %copy-start) | copy-done | bytes 2097176
  81.4 2.9 %shard_map.94 = (bf16[256,1024]{1,0:T(8,128)(2,1)}, bf16[256,1024]{1,0:T(8,128)(2,1)}, bf16[256,1024]{1,0:T(8,128)(2,1)}, bf16[256,1024]{1,0:T(8,128)(2,1)}) custom-call(bf16[4,256,1024]{2,1,0:T(8,128)(2,1)} %copy-done), custom_call_target="tpu_custom_call" | custom-call | tf_op jit(solution)/shard_map/pallas_call | solution.py:542
Async XLA Ops:
  80.1 1.3 %copy-start = (bf16[4,256,1024]{2,1,0:T(8,128)(2,1)}, bf16[4,256,1024]{2,1,0:T(8,128)(2,1)S(1)}, u32[]{:S(2)}) copy-start(bf16[4,256,1024]{2,1,0:T(8,128)(2,1)S(1)} %shard_map.93.stage) | copy-start | bytes 6291460

commit v4 on v3

--- a/solution.py
+++ b/solution.py
@@ -17,8 +17,9 @@
 ONE = 8
 TWO = 4
 MID = (-3, -2, 2, 3)
+LAG = 3
 FG_STEPS = (3, -1, 3, 2, 1)
-Z_STEPS = {1: 1, 2: 2, 3: 3, 4: 1, 5: 2, 6: 3, 7: -1}
+Z_STEPS = {1: 1, 2: 2, 3: 3, 4: 1, 5: 2, 6: 3}
 MID_ROWS = len(MID) * ONE
 FAR_ROWS = (Z - 1) * Y * TWO
 COARSE = MID_ROWS + FAR_ROWS
@@ -45,21 +46,23 @@
 
 
 def kernel(
-    groups, parts,
-    q_hbm, k_hbm, v_hbm, do_hbm, r1_ref, r2_ref,
+    groups, parts, z_parts,
+    q_hbm, k_hbm, v_hbm, do_hbm, r1_hbm, r2_hbm,
     stage,
     own_in, near_kv, near_send, near_recv, own_grad, coarse,
     c1_send, c1_recv, c2_send, c2_recv, z_send, mg_send, mg_recv, fg_send, fg_recv, yg_send, yg_recv,
-    fg_own, restrict, pack, gathered, bias, q_stack, do_stack, key_t, value_t, do_t, score, dots, prob, grad,
+    fg_own, r1_in, r2_in, restrict, pack, gathered, bias, q_stack, do_stack, key_t, value_t, do_t, score, dots, prob, grad,
     att_t, gq_t, coarse_sum, restrict_t,
     load_sem, near_send_sem, near_recv_sem, grad_send_sem, grad_recv_sem,
-    c1_send_sem, c1_recv_sem, c2_send_sem, c2_recv_sem, z_send_sem, z_recv_sem,
+    c1_send_sem, c1_recv_sem, c2_send_sem, c2_recv_sem, z_send_sem, z_recv_sem, z_back_sem,
     mg_send_sem, mg_recv_sem, fg_send_sem, fg_recv_sem, yg_send_sem, yg_recv_sem, go_sem,
 ):
     width = groups * PAIR
     half = width // 2
     part_groups = groups // parts
     part_width = width // parts
+    z_groups = groups // z_parts
+    z_width = width // z_parts
     me = lax.axis_index("seq")
     z = me // Y
     y = me % Y
@@ -87,6 +90,8 @@
         pltpu.make_async_copy(src, own_in.at[i], load_sem.at[i])
         for i, src in enumerate((k_hbm, v_hbm, q_hbm, do_hbm))
     ]
+    loads.append(pltpu.make_async_copy(r1_hbm, r1_in, load_sem.at[4]))
+    loads.append(pltpu.make_async_copy(r2_hbm, r2_in, load_sem.at[5]))
     for load in loads:
         load.start()
 
@@ -114,8 +119,10 @@
         send_near(side, 0, 0)
 
     restrict[...] = jnp.zeros_like(restrict)
-    restrict[0:ONE, :] = r1_ref[...].astype(F32)
-    restrict[ONE:ONE + TWO, :] = r2_ref[...].astype(F32)
+    loads[4].wait()
+    loads[5].wait()
+    restrict[0:ONE, :] = r1_in[...].astype(F32)
+    restrict[ONE:ONE + TWO, :] = r2_in[...].astype(F32)
     restrict_b = restrict[...].astype(BF16)
     restrict_t[...] = restrict[...].T.astype(BF16)
     loads[0].wait()
@@ -194,16 +201,24 @@
     def far_slot(k):
         return pl.ds(MID_ROWS + (k - 1) * Y * TWO, Y * TWO)
 
+    z_back = remote(z_send, coarse.at[:, far_slot(7), :], z_back_sem.at[0], z_back_sem.at[1], at_z(-way))
+    z_back.start()
+
     def z_copy(k, part):
-        cols = columns(part, part_width)
-        src = coarse.at[:, far_slot(3), cols] if k in (4, 5, 6) else z_send.at[:, :, cols]
+        cols = columns(part, z_width)
+        src = coarse.at[:, far_slot(3), cols] if k > 3 else z_send.at[:, :, cols]
         return remote(
             src, coarse.at[:, far_slot(k), cols],
-            z_send_sem.at[part, k - 1], z_recv_sem.at[part, k - 1], at_z(way * Z_STEPS[k]),
+            z_send_sem.at[k - 1, part], z_recv_sem.at[k - 1, part], at_z(way * Z_STEPS[k]),
         )
 
     def z_own(part):
-        for k in (3, 2, 1, 7):
+        for k in (3, 2, 1):
+            z_copy(k, part).start()
+
+    def z_forward(part):
+        z_copy(3, part).wait_recv()
+        for k in (6, 5, 4):
             z_copy(k, part).start()
 
     z_own(0)
@@ -219,12 +234,11 @@
         coarse[which, 0:MID_ROWS, :] = jnp.concatenate(rows, axis=0).astype(BF16)
     loads[2].wait()
     loads[3].wait()
-    for part in range(parts):
-        z_copy(3, part).wait_recv()
-        for k in (6, 5, 4):
-            z_copy(k, part).start()
-        if part + 2 < parts:
+    for part in range(2):
+        z_forward(part)
+        if part + 2 < z_parts:
             z_own(part + 2)
+    z_back.wait_recv()
 
     def grad_copy(side, g):
         return remote(
@@ -267,10 +281,14 @@
         cols = columns(g, PAIR)
         part = g // part_groups
 
-        @pl.when(g % part_groups == 0)
+        @pl.when(g % z_groups == 0)
         def _():
-            for k in (1, 2, 4, 5, 6, 7):
-                z_copy(k, part).wait_recv()
+            for k in (1, 2, 4, 5, 6):
+                z_copy(k, g // z_groups).wait_recv()
+
+        @pl.when(g + 2 < z_parts)
+        def _():
+            z_forward(g + 2)
 
         for side in range(2):
             for which in range(2):
@@ -343,14 +361,6 @@
                 dot(prob[first:first + n, :], do_stack[...], 1, 0),
             )
 
-        for side in range(2):
-            dk, dv = key_grads(2 * ROWS * side, ROWS)
-            near_send[side, g, 0:ROWS, :] = dk.astype(BF16)
-            near_send[side, g, ROWS:2 * ROWS, :] = dv.astype(BF16)
-            grad_copy(side, g).start()
-        dk, dv = key_grads(ROWS, ROWS)
-        own_grad[g, 0:ROWS, :] = dk
-        own_grad[g, ROWS:2 * ROWS, :] = dv
         dk, dv = key_grads(NEAR, COARSE)
         for s in range(len(MID)):
             both = jnp.concatenate([dk[s * ONE:(s + 1) * ONE], dv[s * ONE:(s + 1) * ONE]], axis=0)
@@ -361,11 +371,19 @@
             fg_own[k - 1, 1, :, cols] = dv[first:first + Y * TWO]
         sum_first(g)
 
-        @pl.when(g > 0)
+        @pl.when(g >= LAG)
         def _():
-            sum_second(g - 1)
-
-
+            sum_second(g - LAG)
+
+
+        for side in range(2):
+            dk, dv = key_grads(2 * ROWS * side, ROWS)
+            near_send[side, g, 0:ROWS, :] = dk.astype(BF16)
+            near_send[side, g, ROWS:2 * ROWS, :] = dv.astype(BF16)
+            grad_copy(side, g).start()
+        dk, dv = key_grads(ROWS, ROWS)
+        own_grad[g, 0:ROWS, :] = dk
+        own_grad[g, ROWS:2 * ROWS, :] = dv
         @pl.when(g % part_groups == part_groups - 1)
         def _():
             for s in range(len(MID)):
@@ -385,10 +403,8 @@
             fg_copy(i, g).wait_recv()
         return carry
 
-    sum_second(groups - 1)
-    early = groups - 2
-    for g in range(early):
-        add_near(g)
+    for g in range(max(groups - LAG, 0), groups):
+        sum_second(g)
     lax.fori_loop(0, groups, far_arrival, 0)
     for which in range(2):
         total = fg_recv[3, which].astype(F32)
@@ -402,6 +418,9 @@
     for j in range(1, Y):
         yg_send[j - 1] = pack_rows(TWO * j)
         yg_copies[j - 1].start()
+    early = max(groups - 2, 0)
+    for g in range(early):
+        add_near(g)
     for part in range(parts):
         for s in range(len(MID)):
             mg_copy(s, part).wait_recv()
@@ -423,6 +442,7 @@
                     coarse_sum[which, ONE:ONE + TWO, cols] + pack[first:first + TWO, :]
                 )
 
+
     for g in range(early, groups):
         add_near(g)
 
@@ -449,6 +469,10 @@
         return carry
 
     lax.fori_loop(0, groups, drain, 0)
+    z_back.wait_send()
+    for part in range(z_parts):
+        for k in range(1, Z - 1):
+            z_copy(k, part).wait_send()
     for side in range(2):
         @pl.when(jnp.logical_not(wraps[side]))
         def _(side=side):
@@ -457,8 +481,6 @@
     for copy in c1_copies + c2_copies + yg_copies:
         copy.wait_send()
     for part in range(parts):
-        for k in range(1, Z):
-            z_copy(k, part).wait_send()
         for s in range(len(MID)):
             mg_copy(s, part).wait_send()
 
@@ -476,7 +498,8 @@
 def per_device(queries, keys, values, cotangent, restrict_one, restrict_two):
     rows, width = queries.shape
     groups = width // PAIR
-    parts = 4 if groups % 4 == 0 else 2
+    parts = 2
+    z_parts = min(groups, 4)
     shape = jax.ShapeDtypeStruct((rows, width), BF16)
     hbm = pl.BlockSpec(memory_space=pl.ANY)
     vmem = pl.BlockSpec(memory_space=pltpu.VMEM)
@@ -501,6 +524,8 @@
         pltpu.VMEM((Y - 1, 16, width // 2), BF16),
         pltpu.VMEM((Y - 1, 16, width // 2), BF16),
         pltpu.VMEM((Z - 1, 2, 16, width), F32),
+        pltpu.VMEM((ONE, ROWS), BF16),
+        pltpu.VMEM((TWO, ROWS), BF16),
         pltpu.VMEM((16, ROWS), F32),
         pltpu.VMEM((16, width // 2), F32),
         pltpu.VMEM((2, 16, width), F32),
@@ -518,21 +543,21 @@
         pltpu.VMEM((PAIR, ROWS), F32),
         pltpu.VMEM((2, 16, width), F32),
         pltpu.VMEM((ROWS, 16), BF16),
-        dma((4,)),
+        dma((6,)),
         dma((2, 2, groups)), dma((2, 2, groups)),
         dma((2, groups)), dma((2, groups)),
         dma((mid,)), dma((mid,)),
         dma((Y - 1,)), dma((Y - 1,)),
-        dma((parts, Z - 1)), dma((parts, Z - 1)),
+        dma((Z - 2, z_parts)), dma((Z - 2, z_parts)), dma((2,)),
         dma((parts, mid)), dma((parts, mid)),
         dma((5, groups)), dma((5, groups)),
         dma((Y - 1,)), dma((Y - 1,)),
         pltpu.SemaphoreType.REGULAR((2,)),
     ]
     stage = pl.pallas_call(
-        functools.partial(kernel, groups, parts),
+        functools.partial(kernel, groups, parts, z_parts),
         out_shape=pltpu.VMEM((4, ROWS, width), BF16),
-        in_specs=[hbm] * 4 + [vmem] * 2,
+        in_specs=[hbm] * 6,
         out_specs=vmem,
         scratch_shapes=scratch,
         compiler_params=pltpu.CompilerParams(

time: 84.6 us -> 77.3 us (0.914)
  Pallas kernels: 82.4 us -> 75.2 us
    pallas_call x1, Pallas kernels: 79.4 us -> 72.3 us  [per_device(): pl.pallas_call(functools.partial(kernel, groups, parts, z_parts), out_sha...]
where the time goes in v4:
time: 77.3 us; the launch traced here: 77.2 us
  Pallas kernels  75.2 us (97%)
  local copies, waits for them, and re-layouts  1.34 us (2%)
    pallas_call x1, Pallas kernels, per_device(): pl.pallas_call(functools.partial(kernel, groups, parts, z_parts), out_sha...  72.3 us
    pallas_call x1, Pallas kernels, per_device(): pl.pallas_call(write_out, out_shape=[shape] * 4, in_specs=[vmem], out_spe...  2.93 us

profile of v4, /device:TPU:2, one launch (start us, length us, event | category | flops | bytes accessed | tf_op | source)
XLA Modules:
  0.0 77.2 jit_solution(7132454148389494127)
XLA Ops:
  0.6 72.3 %shard_map.93.stage = bf16[4,256,1024]{2,1,0:T(8,128)(2,1)S(1)} custom-call(bf16[256,1024]{1,0:T(8,128)(2,1)} %q_hbm.1, bf16[256,1024]{1,0:T(8,128)(2,1)} %k_hbm.1, bf16[256,1024]{1,0:T(8,128)(2,1)} %v_hbm.1, bf16[256,1024]{1,0:T(8,128)(2,1)} %do_hbm.1, bf16[8,256]{1,0:T(8,128)(2,1)} %r1_hbm.1, bf16[4,256]{1,0:T(4,128)(2,1)} %r2_hbm.1), custom_call_target="tpu_custom_call" | custom-call | tf_op jit(solution)/shard_map/pallas_call | solution.py:557
  72.9 0.0 copy-start
  72.9 1.3 %copy-done = bf16[4,256,1024]{2,1,0:T(8,128)(2,1)} copy-done((bf16[4,256,1024]{2,1,0:T(8,128)(2,1)}, bf16[4,256,1024]{2,1,0:T(8,128)(2,1)S(1)}, u32[]{:S(2)}) %copy-start) | copy-done | bytes 2097176
  74.3 2.9 %shard_map.94 = (bf16[256,1024]{1,0:T(8,128)(2,1)}, bf16[256,1024]{1,0:T(8,128)(2,1)}, bf16[256,1024]{1,0:T(8,128)(2,1)}, bf16[256,1024]{1,0:T(8,128)(2,1)}) custom-call(bf16[4,256,1024]{2,1,0:T(8,128)(2,1)} %copy-done), custom_call_target="tpu_custom_call" | custom-call | tf_op jit(solution)/shard_map/pallas_call | solution.py:567
Async XLA Ops:
  72.9 1.3 %copy-start = (bf16[4,256,1024]{2,1,0:T(8,128)(2,1)}, bf16[4,256,1024]{2,1,0:T(8,128)(2,1)S(1)}, u32[]{:S(2)}) copy-start(bf16[4,256,1024]{2,1,0:T(8,128)(2,1)S(1)} %shard_map.93.stage) | copy-start | bytes 6291460

commit v5 on v4

--- a/solution.py
+++ b/solution.py
@@ -18,6 +18,7 @@
 TWO = 4
 MID = (-3, -2, 2, 3)
 LAG = 3
+LEAD = 4
 FG_STEPS = (3, -1, 3, 2, 1)
 Z_STEPS = {1: 1, 2: 2, 3: 3, 4: 1, 5: 2, 6: 3}
 MID_ROWS = len(MID) * ONE
@@ -51,11 +52,11 @@
     stage,
     own_in, near_kv, near_send, near_recv, own_grad, coarse,
     c1_send, c1_recv, c2_send, c2_recv, z_send, mg_send, mg_recv, fg_send, fg_recv, yg_send, yg_recv,
-    fg_own, r1_in, r2_in, restrict, pack, gathered, bias, q_stack, do_stack, key_t, value_t, do_t, score, dots, prob, grad,
+    fg_own, r1_in, r2_in, restrict, pack, gathered, bias, q_stack, do_stack, key_t, value_t, do_t, score, dots, stats, prob, grad,
     att_t, gq_t, coarse_sum, restrict_t,
     load_sem, near_send_sem, near_recv_sem, grad_send_sem, grad_recv_sem,
     c1_send_sem, c1_recv_sem, c2_send_sem, c2_recv_sem, z_send_sem, z_recv_sem, z_back_sem,
-    mg_send_sem, mg_recv_sem, fg_send_sem, fg_recv_sem, yg_send_sem, yg_recv_sem, go_sem,
+    mg_send_sem, mg_recv_sem, fg_send_sem, fg_recv_sem, yg_send_sem, yg_recv_sem,
 ):
     width = groups * PAIR
     half = width // 2
@@ -142,25 +143,82 @@
     c2_send[...] = pack_rows(ONE)
     c1_send[...] = jnp.concatenate([coarse_k[0:ONE], coarse_v[0:ONE]], axis=0).astype(BF16)
 
-    c2_copies = [
-        remote(c2_send, c2_recv.at[j - 1], c2_send_sem.at[j - 1], c2_recv_sem.at[j - 1], at_y(j))
-        for j in range(1, Y)
-    ]
-    for copy in c2_copies:
-        copy.start()
-    c1_copies = [
-        remote(c1_send, c1_recv.at[s], c1_send_sem.at[s], c1_recv_sem.at[s], at_block(-o))
-        for s, o in enumerate(MID)
-    ]
-    for copy in c1_copies:
-        copy.start()
-
-    wraps = (y == Y - 1, y == 0)
+    first_y, last_y, relay = y == 0, y == Y - 1, (y == 1) | (y == 2)
+    same_z = 2 - y // 2
+
+    def c2_copy(j):
+        return remote(c2_send, c2_recv.at[j - 1], c2_send_sem.at[j - 1], c2_recv_sem.at[j - 1], at_y(j))
+
+    def c1_copy(i):
+        to, slot = ((at_y(2), 3 - same_z), (at_block(3), 0), (at_block(-3), 3))[i]
+        return remote(c1_send, c1_recv.at[slot], c1_send_sem.at[i], c1_recv_sem.at[slot], to)
+
+    def c1_on_z():
+        slot = 3 - same_z
+        return remote(
+            c1_recv.at[same_z], c1_recv.at[slot], c1_send_sem.at[3], c1_recv_sem.at[slot], at_z(way)
+        )
+
+    def c2_on_y():
+        slot = 2 * (y - 1)
+        return remote(c2_recv.at[1], c2_recv.at[slot], c2_send_sem.at[3], c2_recv_sem.at[slot], at_y(2 * y - 3))
+
+    def c1_on_y():
+        slot = 3 * (2 - y)
+        return remote(
+            c1_recv.at[same_z], c1_recv.at[slot], c1_send_sem.at[4], c1_recv_sem.at[slot], at_y(2 * y - 3)
+        )
+
+    def small_copies(act):
+        act(c2_copy(2))
+        act(c1_copy(0))
+
+        @pl.when(jnp.logical_not(first_y))
+        def _():
+            act(c2_copy(3))
+            act(c1_copy(1))
+
+        @pl.when(jnp.logical_not(last_y))
+        def _():
+            act(c2_copy(1))
+            act(c1_copy(2))
+
+    small_copies(lambda copy: copy.start())
+
+    held = (y == 2, y == 1)
+    on_z = (last_y, first_y)
+    some = min(4, groups)
     for side in range(2):
-        @pl.when(jnp.logical_not(wraps[side]))
+        send_near(side, 1, 0)
+
+        @pl.when(jnp.logical_not(held[side]))
         def _(side=side):
-            lax.fori_loop(1, groups, functools.partial(send_near, side), 0)
-
+            lax.fori_loop(2, some, functools.partial(send_near, side), 0)
+
+        @pl.when(jnp.logical_not(held[side] | on_z[side]))
+        def _(side=side):
+            lax.fori_loop(some, groups, functools.partial(send_near, side), 0)
+
+    def c2_arrival(j):
+        remote(c2_send, c2_recv.at[j - 1], c2_send_sem.at[j - 1], c2_recv_sem.at[j - 1], at_y(j)).wait_recv()
+
+    def c1_arrival(slot):
+        remote(c1_send, c1_recv.at[slot], c1_send_sem.at[0], c1_recv_sem.at[slot], at_y(2)).wait_recv()
+
+    c2_arrival(2)
+    c1_arrival(same_z)
+
+    @pl.when(relay)
+    def _():
+        c2_on_y().start()
+        c1_on_y().start()
+
+    for side in range(2):
+        @pl.when(held[side])
+        def _(side=side):
+            lax.fori_loop(2, groups, functools.partial(send_near, side), 0)
+
+    c1_on_z().start()
     row = lax.broadcasted_iota(jnp.int32, (COARSE, ROWS), 0)
     slot = row >> 3
     offset = jnp.where(slot == 0, -3, jnp.where(slot == 1, -2, jnp.where(slot == 2, 2, 3)))
@@ -179,12 +237,8 @@
     prob[KEYS:PADDED, :] = jnp.zeros((PADDED - KEYS, 2 * ROWS), BF16)
     grad[KEYS:PADDED, :] = jnp.zeros((PADDED - KEYS, 2 * ROWS), BF16)
 
-    for copy in c2_copies + c1_copies:
-        copy.wait_recv()
-    for side in range(2):
-        pl.semaphore_signal(
-            go_sem.at[side], inc=1, device_id={"seq": at_block(-1 if side == 0 else 1)}, device_id_type=MESH
-        )
+    c2_arrival(1)
+    c2_arrival(3)
 
     for j in range(Y):
         if j == 0:
@@ -203,6 +257,10 @@
 
     z_back = remote(z_send, coarse.at[:, far_slot(7), :], z_back_sem.at[0], z_back_sem.at[1], at_z(-way))
     z_back.start()
+    for side in range(2):
+        @pl.when(on_z[side])
+        def _(side=side):
+            lax.fori_loop(some, groups, functools.partial(send_near, side), 0)
 
     def z_copy(k, part):
         cols = columns(part, z_width)
@@ -223,23 +281,13 @@
 
     z_own(0)
     z_own(1)
-    for side in range(2):
-        @pl.when(wraps[side])
-        def _(side=side):
-            pl.semaphore_wait(go_sem.at[side], 1)
-            lax.fori_loop(1, groups, functools.partial(send_near, side), 0)
-
+    for slot in (0, 3, 3 - same_z):
+        c1_arrival(slot)
     for which in range(2):
         rows = [c1_recv[s].astype(F32)[which * ONE:(which + 1) * ONE] for s in range(len(MID))]
         coarse[which, 0:MID_ROWS, :] = jnp.concatenate(rows, axis=0).astype(BF16)
     loads[2].wait()
     loads[3].wait()
-    for part in range(2):
-        z_forward(part)
-        if part + 2 < z_parts:
-            z_own(part + 2)
-    z_back.wait_recv()
-
     def grad_copy(side, g):
         return remote(
             near_send.at[side, g], near_recv.at[1 - side, g],
@@ -277,88 +325,109 @@
             fg_send[4 + i, :, :, cols] = total.astype(BF16)
             fg_copy(2 + i, g).start()
 
-    def pair(g, carry):
+    def heads(g):
         cols = columns(g, PAIR)
-        part = g // part_groups
-
-        @pl.when(g % z_groups == 0)
-        def _():
-            for k in (1, 2, 4, 5, 6):
-                z_copy(k, g // z_groups).wait_recv()
-
-        @pl.when(g + 2 < z_parts)
-        def _():
-            z_forward(g + 2)
-
+        return lax.rem(g, LEAD), cols, own_in[2, :, cols], own_in[3, :, cols]
+
+    def near_part(g):
+        slot, cols, q, do = heads(g)
         for side in range(2):
             for which in range(2):
                 near_copy(side, which, g).wait_recv()
-
-        def key_value(which):
-            first = which * ROWS
-            return (
-                near_kv[0, g, first:first + ROWS, :],
-                own_in[which, :, cols],
-                near_kv[1, g, first:first + ROWS, :],
-                coarse[which, :, cols],
-            )
-
-        q = own_in[2, :, cols].astype(F32) * (1.0 / math.sqrt(HEAD_DIM))
-        do = own_in[3, :, cols].astype(F32)
+        q = q.astype(F32) * (1.0 / math.sqrt(HEAD_DIM))
+        do = do.astype(F32)
         lane = lax.broadcasted_iota(jnp.int32, (ROWS, PAIR), 1)
         for h in range(2):
             mine = (lane >= HEAD_DIM) if h else (lane < HEAD_DIM)
-            q_stack[h * ROWS:(h + 1) * ROWS, :] = jnp.where(mine, q, 0.0).astype(BF16)
-            do_stack[h * ROWS:(h + 1) * ROWS, :] = jnp.where(mine, do, 0.0).astype(BF16)
-        do_t[...] = do.T
-        keys = key_value(0)
-        values = key_value(1)
-        for i in range(4):
-            key_t[:, i * ROWS:(i + 1) * ROWS] = keys[i].T
-            value_t[:, i * ROWS:(i + 1) * ROWS] = values[i].T
-        counts = (ROWS, ROWS, ROWS, COARSE)
-        biases = (left_bias, None, right_bias, bias)
+            q_stack[slot, h * ROWS:(h + 1) * ROWS, :] = jnp.where(mine, q, 0.0).astype(BF16)
+            do_stack[slot, h * ROWS:(h + 1) * ROWS, :] = jnp.where(mine, do, 0.0).astype(BF16)
+        do_t[slot] = do.T
+        keys, values = (
+            (
+                near_kv[0, g, which * ROWS:(which + 1) * ROWS, :],
+                own_in[which, :, cols],
+                near_kv[1, g, which * ROWS:(which + 1) * ROWS, :],
+            )
+            for which in range(2)
+        )
+        for i in range(3):
+            key_t[slot, :, i * ROWS:(i + 1) * ROWS] = keys[i].T
+            value_t[slot, :, i * ROWS:(i + 1) * ROWS] = values[i].T
+        biases = (left_bias, None, right_bias)
         for h in range(2):
-            qh = q_stack[h * ROWS:(h + 1) * ROWS, :]
-            doh = do_stack[h * ROWS:(h + 1) * ROWS, :]
-            lanes = slice(h * ROWS, (h + 1) * ROWS)
+            qh = q_stack[slot, h * ROWS:(h + 1) * ROWS, :]
+            doh = do_stack[slot, h * ROWS:(h + 1) * ROWS, :]
             top = None
-            for i in range(4):
-                n = counts[i]
-                s = dot(keys[i][:n], qh, 1, 1)
-                if i == 3:
-                    s = s + bias[...]
-                elif biases[i] is not None:
+            for i in range(3):
+                s = dot(keys[i], qh, 1, 1)
+                if biases[i] is not None:
                     s = s + biases[i]
-                score[h, i * ROWS:i * ROWS + n, :] = s
+                score[slot, h, i * ROWS:(i + 1) * ROWS, :] = s
                 m = group_max(s)
                 top = m if top is None else jnp.maximum(top, m)
-                dots[h, i * ROWS:i * ROWS + n, :] = dot(values[i][:n], doh, 1, 1)
+                dots[slot, h, i * ROWS:(i + 1) * ROWS, :] = dot(values[i], doh, 1, 1)
             top = jnp.max(top, axis=0, keepdims=True)
             total = jnp.zeros((8, ROWS), F32)
+            for c in range(0, NEAR, CHUNK):
+                p = jnp.exp(score[slot, h, c:c + CHUNK, :] - top)
+                score[slot, h, c:c + CHUNK, :] = p
+                total = total + group_sum(p)
+            stats[slot, h, 0] = jnp.broadcast_to(top, (8, ROWS))
+            stats[slot, h, 1] = total
+
+    def pair(g):
+        slot, cols, _, _ = heads(g)
+        part = g // part_groups
+
+        @pl.when(g == 0)
+        def _():
+            z_back.wait_recv()
+
+        @pl.when(g % z_groups == 0)
+        def _():
+            for k in (1, 2, 4, 5, 6):
+                z_copy(k, g // z_groups).wait_recv()
+
+        @pl.when(g + 2 < z_parts)
+        def _():
+            z_forward(g + 2)
+
+        key = coarse[0, :, cols]
+        value = coarse[1, :, cols]
+        key_t[slot, :, NEAR:PADDED] = key.T
+        value_t[slot, :, NEAR:PADDED] = value.T
+        for h in range(2):
+            qh = q_stack[slot, h * ROWS:(h + 1) * ROWS, :]
+            doh = do_stack[slot, h * ROWS:(h + 1) * ROWS, :]
+            lanes = slice(h * ROWS, (h + 1) * ROWS)
+            s = dot(key[:COARSE], qh, 1, 1) + bias[...]
+            dots[slot, h, NEAR:KEYS, :] = dot(value[:COARSE], doh, 1, 1)
+            near_top = stats[slot, h, 0, 0:1, :]
+            top = jnp.maximum(near_top, jnp.max(group_max(s), axis=0, keepdims=True))
+            p = jnp.exp(s - top)
+            score[slot, h, NEAR:KEYS, :] = p
+            shrink = jnp.exp(near_top - top)
+            total = shrink * jnp.sum(stats[slot, h, 1], axis=0, keepdims=True)
+            inverse = 1.0 / (total + jnp.sum(group_sum(p), axis=0, keepdims=True))
+            near_inverse = shrink * inverse
             for c in range(0, KEYS, CHUNK):
-                p = jnp.exp(score[h, c:c + CHUNK, :] - top)
-                score[h, c:c + CHUNK, :] = p
-                total = total + group_sum(p)
-            inverse = 1.0 / jnp.sum(total, axis=0, keepdims=True)
-            for c in range(0, KEYS, CHUNK):
-                p = score[h, c:c + CHUNK, :] * inverse
+                p = score[slot, h, c:c + CHUNK, :] * (near_inverse if c < NEAR else inverse)
                 prob[c:c + CHUNK, lanes] = p.astype(BF16)
             head = slice(h * HEAD_DIM, (h + 1) * HEAD_DIM)
-            att = dot(value_t[head, :], prob[:, lanes], 1, 0).astype(BF16).astype(F32)
+            att = dot(value_t[slot, head, :], prob[:, lanes], 1, 0).astype(BF16).astype(F32)
             att_t[head, :] = att
-            delta = jnp.sum(att * do_t[head, :], axis=0, keepdims=True)
+            delta = jnp.sum(att * do_t[slot, head, :], axis=0, keepdims=True)
             for c in range(0, KEYS, CHUNK):
-                p = score[h, c:c + CHUNK, :] * inverse
-                grad[c:c + CHUNK, lanes] = (p * (dots[h, c:c + CHUNK, :] - delta)).astype(BF16)
-            gq_t[head, :] = dot(key_t[head, :], grad[:, lanes], 1, 0) * (1.0 / math.sqrt(HEAD_DIM))
+                p = score[slot, h, c:c + CHUNK, :] * (near_inverse if c < NEAR else inverse)
+                grad[c:c + CHUNK, lanes] = (p * (dots[slot, h, c:c + CHUNK, :] - delta)).astype(BF16)
+            gq_t[head, :] = dot(key_t[slot, head, :], grad[:, lanes], 1, 0) * (1.0 / math.sqrt(HEAD_DIM))
         stage[0, :, cols] = att_t[...].T.astype(BF16)
         stage[1, :, cols] = gq_t[...].T.astype(BF16)
 
         def key_grads(first, n):
             return (
-                dot(grad[first:first + n, :], q_stack[...], 1, 0),
-                dot(prob[first:first + n, :], do_stack[...], 1, 0),
+                dot(grad[first:first + n, :], q_stack[slot], 1, 0),
+                dot(prob[first:first + n, :], do_stack[slot], 1, 0),
             )
 
         dk, dv = key_grads(NEAR, COARSE)
@@ -376,6 +445,11 @@
             sum_second(g - LAG)
 
 
+        @pl.when(g % part_groups == part_groups - 1)
+        def _():
+            for s in range(len(MID)):
+                mg_copy(s, part).start()
+
         for side in range(2):
             dk, dv = key_grads(2 * ROWS * side, ROWS)
             near_send[side, g, 0:ROWS, :] = dk.astype(BF16)
@@ -384,14 +458,27 @@
         dk, dv = key_grads(ROWS, ROWS)
         own_grad[g, 0:ROWS, :] = dk
         own_grad[g, ROWS:2 * ROWS, :] = dv
-        @pl.when(g % part_groups == part_groups - 1)
-        def _():
-            for s in range(len(MID)):
-                mg_copy(s, part).start()
+    lead = min(LEAD, groups)
+
+    def turn(t, carry):
+        @pl.when(t >= lead)
+        def _():
+            pair(t - lead)
+
+        @pl.when(t < groups)
+        def _():
+            near_part(t)
+
+        for part in range(2):
+            @pl.when(t == min(part + 1, lead - 1))
+            def _(part=part):
+                z_forward(part)
+                if part + 2 < z_parts:
+                    z_own(part + 2)
 
         return carry
 
-    lax.fori_loop(0, groups, pair, 0)
+    lax.fori_loop(0, groups + lead, turn, 0)
 
     def add_near(g):
         for side in range(2):
@@ -473,26 +560,19 @@
     for part in range(z_parts):
         for k in range(1, Z - 1):
             z_copy(k, part).wait_send()
-    for side in range(2):
-        @pl.when(jnp.logical_not(wraps[side]))
-        def _(side=side):
-            pl.semaphore_wait(go_sem.at[side], 1)
-
-    for copy in c1_copies + c2_copies + yg_copies:
+    for copy in yg_copies:
         copy.wait_send()
+    small_copies(lambda copy: copy.wait_send())
+    c1_on_z().wait_send()
+
+    @pl.when(relay)
+    def _():
+        c2_on_y().wait_send()
+        c1_on_y().wait_send()
+
     for part in range(parts):
         for s in range(len(MID)):
             mg_copy(s, part).wait_send()
-
-
-def write_out(stage, att, gq, gk, gv, sem):
-    copies = [
-        pltpu.make_async_copy(stage.at[i], out, sem.at[i]) for i, out in enumerate((att, gq, gk, gv))
-    ]
-    for copy in copies:
-        copy.start()
-    for copy in copies:
-        copy.wait()
 
 
 def per_device(queries, keys, values, cotangent, restrict_one, restrict_two):
@@ -500,7 +580,6 @@
     groups = width // PAIR
     parts = 2
     z_parts = min(groups, 4)
-    shape = jax.ShapeDtypeStruct((rows, width), BF16)
     hbm = pl.BlockSpec(memory_space=pl.ANY)
     vmem = pl.BlockSpec(memory_space=pltpu.VMEM)
     dma = pltpu.SemaphoreType.DMA
@@ -530,13 +609,14 @@
         pltpu.VMEM((16, width // 2), F32),
         pltpu.VMEM((2, 16, width), F32),
         pltpu.VMEM((COARSE, ROWS), F32),
-        pltpu.VMEM((2 * ROWS, PAIR), BF16),
-        pltpu.VMEM((2 * ROWS, PAIR), BF16),
-        pltpu.VMEM((PAIR, PADDED), BF16),
-        pltpu.VMEM((PAIR, PADDED), BF16),
-        pltpu.VMEM((PAIR, ROWS), F32),
-        pltpu.VMEM((2, KEYS, ROWS), F32),
-        pltpu.VMEM((2, KEYS, ROWS), F32),
+        pltpu.VMEM((LEAD, 2 * ROWS, PAIR), BF16),
+        pltpu.VMEM((LEAD, 2 * ROWS, PAIR), BF16),
+        pltpu.VMEM((LEAD, PAIR, PADDED), BF16),
+        pltpu.VMEM((LEAD, PAIR, PADDED), BF16),
+        pltpu.VMEM((LEAD, PAIR, ROWS), F32),
+        pltpu.VMEM((LEAD, 2, KEYS, ROWS), F32),
+        pltpu.VMEM((LEAD, 2, KEYS, ROWS), F32),
+        pltpu.VMEM((LEAD, 2, 2, 8, ROWS), F32),
         pltpu.VMEM((PADDED, 2 * ROWS), BF16),
         pltpu.VMEM((PADDED, 2 * ROWS), BF16),
         pltpu.VMEM((PAIR, ROWS), F32),
@@ -546,13 +626,12 @@
         dma((6,)),
         dma((2, 2, groups)), dma((2, 2, groups)),
         dma((2, groups)), dma((2, groups)),
-        dma((mid,)), dma((mid,)),
-        dma((Y - 1,)), dma((Y - 1,)),
+        dma((5,)), dma((mid,)),
+        dma((4,)), dma((Y - 1,)),
         dma((Z - 2, z_parts)), dma((Z - 2, z_parts)), dma((2,)),
         dma((parts, mid)), dma((parts, mid)),
         dma((5, groups)), dma((5, groups)),
         dma((Y - 1,)), dma((Y - 1,)),
-        pltpu.SemaphoreType.REGULAR((2,)),
     ]
     stage = pl.pallas_call(
         functools.partial(kernel, groups, parts, z_parts),
@@ -564,13 +643,7 @@
             collective_id=0, has_side_effects=True, vmem_limit_bytes=56 * 1024 * 1024
         ),
     )(queries, keys, values, cotangent, restrict_one, restrict_two)
-    return pl.pallas_call(
-        write_out,
-        out_shape=[shape] * 4,
-        in_specs=[vmem],
-        out_specs=[hbm] * 4,
-        scratch_shapes=[dma((4,))],
-    )(stage)
+    return tuple(stage[i] for i in range(4))
 
 
 def solution(mesh):

time: 77.3 us -> 71.9 us (0.930)
  Pallas kernels: 75.2 us -> 69.9 us
    pallas_call x1 -> x0, Pallas kernels: 2.93 us -> none  [per_device(): pl.pallas_call(write_out, out_shape=[shape] * 4, in_specs=[vmem], out_spe...]
    pallas_call x1, Pallas kernels: 72.3 us -> 69.9 us  [per_device(): pl.pallas_call(functools.partial(kernel, groups, parts, z_parts), out_sha...]
    squeeze x0 -> x1, local copies, waits for them, and re-layouts: none -> 1.35 us  [per_device(): return tuple((stage[i] for i in range(4)))]
    unnamed x2 -> x0, local copies, waits for them, and re-layouts: 1.34 us -> none
where the time goes in v5:
time: 71.9 us
  Pallas kernels  69.9 us (97%)
  local copies, waits for them, and re-layouts  1.35 us (2%)
    pallas_call x1, Pallas kernels, per_device(): pl.pallas_call(functools.partial(kernel, groups, parts, z_parts), out_sha...  69.9 us

profile of v5, /device:TPU:2, one launch (start us, length us, event | category | flops | bytes accessed | tf_op | source)
XLA Modules:
  0.0 71.9 jit_solution(779163267445552946)
XLA Ops:
  0.6 69.9 %shard_map.93 = bf16[4,256,1024]{2,1,0:T(8,128)(2,1)S(1)} custom-call(bf16[256,1024]{1,0:T(8,128)(2,1)} %q_hbm.1, bf16[256,1024]{1,0:T(8,128)(2,1)} %k_hbm.1, bf16[256,1024]{1,0:T(8,128)(2,1)} %v_hbm.1, bf16[256,1024]{1,0:T(8,128)(2,1)} %do_hbm.1, bf16[8,256]{1,0:T(8,128)(2,1)} %r1_hbm.1, bf16[4,256]{1,0:T(4,128)(2,1)} %r2_hbm.1), custom_call_target="tpu_custom_call" | custom-call | tf_op jit(solution)/shard_map/pallas_call | solution.py:636
  70.5 1.3 %slice_bitcast_fusion = (bf16[256,1024]{1,0:T(8,128)(2,1)}, bf16[256,1024]{1,0:T(8,128)(2,1)}, bf16[256,1024]{1,0:T(8,128)(2,1)}, bf16[256,1024]{1,0:T(8,128)(2,1)}) fusion(bf16[4,256,1024]{2,1,0:T(8,128)(2,1)S(1)} %shard_map.93), kind=kLoop, calls=%fused_computation | loop fusion | bytes 4194304 | tf_op jit(solution)/shard_map/squeeze | solution.py:646

commit v6 on v5

--- a/solution.py
+++ b/solution.py
@@ -18,7 +18,7 @@
 TWO = 4
 MID = (-3, -2, 2, 3)
 LAG = 3
-LEAD = 4
+LEAD = 5
 FG_STEPS = (3, -1, 3, 2, 1)
 Z_STEPS = {1: 1, 2: 2, 3: 3, 4: 1, 5: 2, 6: 3}
 MID_ROWS = len(MID) * ONE
@@ -125,7 +125,7 @@
     restrict[0:ONE, :] = r1_in[...].astype(F32)
     restrict[ONE:ONE + TWO, :] = r2_in[...].astype(F32)
     restrict_b = restrict[...].astype(BF16)
-    restrict_t[...] = restrict[...].T.astype(BF16)
+    restrict_t[...] = jnp.concatenate([restrict[...], restrict[...]], axis=0).T.astype(BF16)
     loads[0].wait()
     loads[1].wait()
     coarse_k = dot(restrict_b, own_in[0], 1, 0)
@@ -505,8 +505,29 @@
     for j in range(1, Y):
         yg_send[j - 1] = pack_rows(TWO * j)
         yg_copies[j - 1].start()
-    early = max(groups - 2, 0)
-    for g in range(early):
+
+    def drain(g, carry):
+        for side in range(2):
+            for which in range(2):
+                near_copy(side, which, g).wait_send()
+        for i in range(5):
+            fg_copy(i, g).wait_send()
+        return carry
+
+    lax.fori_loop(0, groups, drain, 0)
+    z_back.wait_send()
+    for part in range(z_parts):
+        for k in range(1, Z - 1):
+            z_copy(k, part).wait_send()
+    small_copies(lambda copy: copy.wait_send())
+    c1_on_z().wait_send()
+
+    @pl.when(relay)
+    def _():
+        c2_on_y().wait_send()
+        c1_on_y().wait_send()
+
+    for g in range(groups):
         add_near(g)
     for part in range(parts):
         for s in range(len(MID)):
@@ -530,46 +551,20 @@
                 )
 
 
-    for g in range(early, groups):
-        add_near(g)
-
-    def finish(g, carry):
-        cols = columns(g, PAIR)
+    for g in range(groups):
+        cols = slice(g * PAIR, (g + 1) * PAIR)
         for which in range(2):
-            rows = slice(which * ROWS, (which + 1) * ROWS)
             wide = coarse_sum[which, :, cols]
             high = wide.astype(BF16)
             low = (wide - high.astype(F32)).astype(BF16)
-            total = own_grad[g, rows, :] + dot(restrict_t[...], high, 1, 0) + dot(restrict_t[...], low, 1, 0)
+            both = jnp.concatenate([high, low], axis=0)
+            total = own_grad[g, which * ROWS:(which + 1) * ROWS, :] + dot(restrict_t[...], both, 1, 0)
             stage[2 + which, :, cols] = total.astype(BF16)
-        return carry
-
-    lax.fori_loop(0, groups, finish, 0)
-
-    def drain(g, carry):
+    for g in range(groups):
         for side in range(2):
-            for which in range(2):
-                near_copy(side, which, g).wait_send()
             grad_copy(side, g).wait_send()
-        for i in range(5):
-            fg_copy(i, g).wait_send()
-        return carry
-
-    lax.fori_loop(0, groups, drain, 0)
-    z_back.wait_send()
-    for part in range(z_parts):
-        for k in range(1, Z - 1):
-            z_copy(k, part).wait_send()
     for copy in yg_copies:
         copy.wait_send()
-    small_copies(lambda copy: copy.wait_send())
-    c1_on_z().wait_send()
-
-    @pl.when(relay)
-    def _():
-        c2_on_y().wait_send()
-        c1_on_y().wait_send()
-
     for part in range(parts):
         for s in range(len(MID)):
             mg_copy(s, part).wait_send()
@@ -622,7 +617,7 @@
         pltpu.VMEM((PAIR, ROWS), F32),
         pltpu.VMEM((PAIR, ROWS), F32),
         pltpu.VMEM((2, 16, width), F32),
-        pltpu.VMEM((ROWS, 16), BF16),
+        pltpu.VMEM((ROWS, 32), BF16),
         dma((6,)),
         dma((2, 2, groups)), dma((2, 2, groups)),
         dma((2, groups)), dma((2, groups)),

time: 71.9 us -> 70.1 us (0.975); the launches traced: 71.9 us -> 69 us
  Pallas kernels: 69.9 us -> 67.1 us
    pallas_call x1, Pallas kernels: 69.9 us -> 67.1 us  [per_device(): pl.pallas_call(functools.partial(kernel, groups, parts, z_parts), out_sha...]
where the time goes in v6:
time: 70.1 us; the launch traced here: 69 us
  Pallas kernels  67.1 us (96%)
  local copies, waits for them, and re-layouts  1.35 us (2%)
    pallas_call x1, Pallas kernels, per_device(): pl.pallas_call(functools.partial(kernel, groups, parts, z_parts), out_sha...  67.1 us

profile of v6, /device:TPU:2, one launch (start us, length us, event | category | flops | bytes accessed | tf_op | source)
XLA Modules:
  0.0 69.0 jit_solution(6777930564223399069)
XLA Ops:
  0.6 67.1 %shard_map.93 = bf16[4,256,1024]{2,1,0:T(8,128)(2,1)S(1)} custom-call(bf16[256,1024]{1,0:T(8,128)(2,1)} %q_hbm.1, bf16[256,1024]{1,0:T(8,128)(2,1)} %k_hbm.1, bf16[256,1024]{1,0:T(8,128)(2,1)} %v_hbm.1, bf16[256,1024]{1,0:T(8,128)(2,1)} %do_hbm.1, bf16[8,256]{1,0:T(8,128)(2,1)} %r1_hbm.1, bf16[4,256]{1,0:T(4,128)(2,1)} %r2_hbm.1), custom_call_target="tpu_custom_call" | custom-call | tf_op jit(solution)/shard_map/pallas_call | solution.py:631
  67.7 1.3 %slice_bitcast_fusion = (bf16[256,1024]{1,0:T(8,128)(2,1)}, bf16[256,1024]{1,0:T(8,128)(2,1)}, bf16[256,1024]{1,0:T(8,128)(2,1)}, bf16[256,1024]{1,0:T(8,128)(2,1)}) fusion(bf16[4,256,1024]{2,1,0:T(8,128)(2,1)S(1)} %shard_map.93), kind=kLoop, calls=%fused_computation | loop fusion | bytes 4194304 | tf_op jit(solution)/shard_map/squeeze | solution.py:641

commit v7 on v6

--- a/solution.py
+++ b/solution.py
@@ -87,6 +87,11 @@
     def columns(index, size):
         return pl.ds(pl.multiple_of(index * size, size), size)
 
+    barrier = pltpu.get_barrier_semaphore()
+    partners = [at_block(o) for o in (-1, 1) + MID]
+    partners += [at_y(j) for j in range(1, Y)] + [at_z(k) for k in (-3, -2, -1, 1, 2, 3)]
+    for partner in partners:
+        pl.semaphore_signal(barrier, inc=1, device_id={"seq": partner}, device_id_type=MESH)
     loads = [
         pltpu.make_async_copy(src, own_in.at[i], load_sem.at[i])
         for i, src in enumerate((k_hbm, v_hbm, q_hbm, do_hbm))
@@ -95,12 +100,6 @@
     loads.append(pltpu.make_async_copy(r2_hbm, r2_in, load_sem.at[5]))
     for load in loads:
         load.start()
-
-    barrier = pltpu.get_barrier_semaphore()
-    partners = [at_block(o) for o in (-1, 1) + MID]
-    partners += [at_y(j) for j in range(1, Y)] + [at_z(k) for k in (-3, -2, -1, 1, 2, 3)]
-    for partner in partners:
-        pl.semaphore_signal(barrier, inc=1, device_id={"seq": partner}, device_id_type=MESH)
     pl.semaphore_wait(barrier, len(partners))
 
     def near_copy(side, which, g):
@@ -420,10 +419,6 @@
             for c in range(0, KEYS, CHUNK):
                 p = score[slot, h, c:c + CHUNK, :] * (near_inverse if c < NEAR else inverse)
                 grad[c:c + CHUNK, lanes] = (p * (dots[slot, h, c:c + CHUNK, :] - delta)).astype(BF16)
-            gq_t[head, :] = dot(key_t[slot, head, :], grad[:, lanes], 1, 0) * (1.0 / math.sqrt(HEAD_DIM))
-        stage[0, :, cols] = att_t[...].T.astype(BF16)
-        stage[1, :, cols] = gq_t[...].T.astype(BF16)
-
         def key_grads(first, n):
             return (
                 dot(grad[first:first + n, :], q_stack[slot], 1, 0),
@@ -458,6 +453,12 @@
         dk, dv = key_grads(ROWS, ROWS)
         own_grad[g, 0:ROWS, :] = dk
         own_grad[g, ROWS:2 * ROWS, :] = dv
+        for h in range(2):
+            head = slice(h * HEAD_DIM, (h + 1) * HEAD_DIM)
+            gq = dot(key_t[slot, head, :], grad[:, h * ROWS:(h + 1) * ROWS], 1, 0)
+            gq_t[head, :] = gq * (1.0 / math.sqrt(HEAD_DIM))
+        stage[0, :, cols] = att_t[...].T.astype(BF16)
+        stage[1, :, cols] = gq_t[...].T.astype(BF16)
     lead = min(LEAD, groups)
 
     def turn(t, carry):

time: 70.1 us -> 68.6 us (0.979)
  Pallas kernels: 67.1 us -> 66.1 us
    pallas_call x1, Pallas kernels: 67.1 us -> 66.1 us  [per_device(): pl.pallas_call(functools.partial(kernel, groups, parts, z_parts), out_sha...]
where the time goes in v7:
time: 68.6 us; the launch traced here: 68.1 us
  Pallas kernels  66.1 us (96%)
  local copies, waits for them, and re-layouts  1.35 us (2%)
    pallas_call x1, Pallas kernels, per_device(): pl.pallas_call(functools.partial(kernel, groups, parts, z_parts), out_sha...  66.1 us

profile of v7, /device:TPU:2, one launch (start us, length us, event | category | flops | bytes accessed | tf_op | source)
XLA Modules:
  0.0 68.1 jit_solution(6795861365221859930)
XLA Ops:
  0.6 66.1 %shard_map.93 = bf16[4,256,1024]{2,1,0:T(8,128)(2,1)S(1)} custom-call(bf16[256,1024]{1,0:T(8,128)(2,1)} %q_hbm.1, bf16[256,1024]{1,0:T(8,128)(2,1)} %k_hbm.1, bf16[256,1024]{1,0:T(8,128)(2,1)} %v_hbm.1, bf16[256,1024]{1,0:T(8,128)(2,1)} %do_hbm.1, bf16[8,256]{1,0:T(8,128)(2,1)} %r1_hbm.1, bf16[4,256]{1,0:T(4,128)(2,1)} %r2_hbm.1), custom_call_target="tpu_custom_call" | custom-call | tf_op jit(solution)/shard_map/pallas_call | solution.py:632
  66.7 1.3 %slice_bitcast_fusion = (bf16[256,1024]{1,0:T(8,128)(2,1)}, bf16[256,1024]{1,0:T(8,128)(2,1)}, bf16[256,1024]{1,0:T(8,128)(2,1)}, bf16[256,1024]{1,0:T(8,128)(2,1)}) fusion(bf16[4,256,1024]{2,1,0:T(8,128)(2,1)S(1)} %shard_map.93), kind=kLoop, calls=%fused_computation | loop fusion | bytes 4194304 | tf_op jit(solution)/shard_map/squeeze | solution.py:642

commit v8 on v7

--- a/solution.py
+++ b/solution.py
@@ -17,7 +17,7 @@
 ONE = 8
 TWO = 4
 MID = (-3, -2, 2, 3)
-LAG = 3
+LAG = 5
 LEAD = 5
 FG_STEPS = (3, -1, 3, 2, 1)
 Z_STEPS = {1: 1, 2: 2, 3: 3, 4: 1, 5: 2, 6: 3}
@@ -440,16 +440,16 @@
             sum_second(g - LAG)
 
 
-        @pl.when(g % part_groups == part_groups - 1)
-        def _():
-            for s in range(len(MID)):
-                mg_copy(s, part).start()
-
         for side in range(2):
             dk, dv = key_grads(2 * ROWS * side, ROWS)
             near_send[side, g, 0:ROWS, :] = dk.astype(BF16)
             near_send[side, g, ROWS:2 * ROWS, :] = dv.astype(BF16)
             grad_copy(side, g).start()
+        @pl.when(g % part_groups == part_groups - 1)
+        def _():
+            for s in range(len(MID)):
+                mg_copy(s, part).start()
+
         dk, dv = key_grads(ROWS, ROWS)
         own_grad[g, 0:ROWS, :] = dk
         own_grad[g, ROWS:2 * ROWS, :] = dv

time: 68.6 us -> 68.1 us (level)
  no operation moved by 1% of the time
where the time goes in v8:
time: 68.1 us; the launch traced here: 67.5 us
  Pallas kernels  65.5 us (96%)
  local copies, waits for them, and re-layouts  1.35 us (2%)
    pallas_call x1, Pallas kernels, per_device(): pl.pallas_call(functools.partial(kernel, groups, parts, z_parts), out_sha...  65.5 us

profile of v8, /device:TPU:2, one launch (start us, length us, event | category | flops | bytes accessed | tf_op | source)
XLA Modules:
  0.0 67.5 jit_solution(6297303332922211435)
XLA Ops:
  0.6 65.5 %shard_map.93 = bf16[4,256,1024]{2,1,0:T(8,128)(2,1)S(1)} custom-call(bf16[256,1024]{1,0:T(8,128)(2,1)} %q_hbm.1, bf16[256,1024]{1,0:T(8,128)(2,1)} %k_hbm.1, bf16[256,1024]{1,0:T(8,128)(2,1)} %v_hbm.1, bf16[256,1024]{1,0:T(8,128)(2,1)} %do_hbm.1, bf16[8,256]{1,0:T(8,128)(2,1)} %r1_hbm.1, bf16[4,256]{1,0:T(4,128)(2,1)} %r2_hbm.1), custom_call_target="tpu_custom_call" | custom-call | tf_op jit(solution)/shard_map/pallas_call | solution.py:632
  66.1 1.3 %slice_bitcast_fusion = (bf16[256,1024]{1,0:T(8,128)(2,1)}, bf16[256,1024]{1,0:T(8,128)(2,1)}, bf16[256,1024]{1,0:T(8,128)(2,1)}, bf16[256,1024]{1,0:T(8,128)(2,1)}) fusion(bf16[4,256,1024]{2,1,0:T(8,128)(2,1)S(1)} %shard_map.93), kind=kLoop, calls=%fused_computation | loop fusion | bytes 4194304 | tf_op jit(solution)/shard_map/squeeze | solution.py:642

commit v9 on v8

--- a/solution.py
+++ b/solution.py
@@ -17,7 +17,7 @@
 ONE = 8
 TWO = 4
 MID = (-3, -2, 2, 3)
-LAG = 5
+LAG = 8
 LEAD = 5
 FG_STEPS = (3, -1, 3, 2, 1)
 Z_STEPS = {1: 1, 2: 2, 3: 3, 4: 1, 5: 2, 6: 3}

time: 68.1 us -> 67.7 us (level)
  no operation moved by 1% of the time
where the time goes in v9:
time: 67.7 us; the launch traced here: 67.6 us
  Pallas kernels  65.6 us (97%)
  local copies, waits for them, and re-layouts  1.35 us (2%)
    pallas_call x1, Pallas kernels, per_device(): pl.pallas_call(functools.partial(kernel, groups, parts, z_parts), out_sha...  65.6 us

profile of v9, /device:TPU:2, one launch (start us, length us, event | category | flops | bytes accessed | tf_op | source)
XLA Modules:
  0.0 67.6 jit_solution(17507566817367901504)
XLA Ops:
  0.6 65.6 %shard_map.93 = bf16[4,256,1024]{2,1,0:T(8,128)(2,1)S(1)} custom-call(bf16[256,1024]{1,0:T(8,128)(2,1)} %q_hbm.1, bf16[256,1024]{1,0:T(8,128)(2,1)} %k_hbm.1, bf16[256,1024]{1,0:T(8,128)(2,1)} %v_hbm.1, bf16[256,1024]{1,0:T(8,128)(2,1)} %do_hbm.1, bf16[8,256]{1,0:T(8,128)(2,1)} %r1_hbm.1, bf16[4,256]{1,0:T(4,128)(2,1)} %r2_hbm.1), custom_call_target="tpu_custom_call" | custom-call | tf_op jit(solution)/shard_map/pallas_call | solution.py:632
  66.3 1.3 %slice_bitcast_fusion = (bf16[256,1024]{1,0:T(8,128)(2,1)}, bf16[256,1024]{1,0:T(8,128)(2,1)}, bf16[256,1024]{1,0:T(8,128)(2,1)}, bf16[256,1024]{1,0:T(8,128)(2,1)}) fusion(bf16[4,256,1024]{2,1,0:T(8,128)(2,1)S(1)} %shard_map.93), kind=kLoop, calls=%fused_computation | loop fusion | bytes 4194304 | tf_op jit(solution)/shard_map/squeeze | solution.py:642
